TPU v7x, 512 devices: a whole 4x8x8 slice. The times are simulated.
512 devices in a mesh: row: 64 (over x, z, core), col: 8 (over y).
Axes of the slice: x: 4, y: 8, z: 8, core: 2. Of those that a mesh axis runs over, the one named last changes fastest.
Arguments:
- matrix: float32 [16384, 16384], P('row', 'col'), as said below
Outputs:
- reduced: float32 [16384, 16384], P('row', 'col')
Inputs may be any that keep to these rules, and one draw needn't show every extreme that they name: matrix is symmetric.
All inputs are finite; a program needn't handle non-finite values.
Results may differ from a plain program's by a relative error of at most 0.00012.
Values sent between devices are 32-bit elements; how exact they have to be, the bound alone decides.
A program may use at most 64 MiB of HBM per device.

v0:
```python
import jax
import jax.numpy as jnp
from jax import lax
from jax.sharding import PartitionSpec as P

B = 96
PANELS = 2


HIGH = lax.Precision.HIGHEST


def broadcast(value, axis, source):
    kept = jnp.where(lax.axis_index(axis) == source, value, 0).astype(value.dtype)
    return lax.psum(kept, axis)


def unit_lower_upper(square):
    size = square.shape[0]
    index = jnp.arange(size)

    def step(k, carry):
        work, multipliers = carry
        pivot_row = lax.dynamic_index_in_dim(work, k, 0, keepdims=False)
        column = lax.dynamic_index_in_dim(work, k, 1, keepdims=False)
        ratio = jnp.where(index > k, column / pivot_row[k], 0.0)
        work = work - ratio[:, None] * pivot_row[None, :]
        multipliers = multipliers + ratio[:, None] * (index[None, :] == k).astype(square.dtype)
        return (work, multipliers)

    work, multipliers = lax.fori_loop(0, size, step, (square, jnp.zeros_like(square)))
    return (multipliers + jnp.eye(size, dtype=square.dtype), jnp.triu(work))


def panel_update(block, start):
    row_count, col_count = block.shape
    row_place = lax.axis_index("row")
    col_place = lax.axis_index("col")
    trail = start + B
    rows = row_place * row_count + jnp.arange(row_count)
    live = (rows >= trail)[:, None]
    panel = broadcast(block[:, start : start + B], "col", 0)
    panel = jnp.where(live, panel, 0.0)
    picker = (rows[None, :] == trail + jnp.arange(B)[:, None]).astype(block.dtype)
    gram, top = lax.psum(
        (jnp.dot(panel.T, panel, precision=HIGH), jnp.dot(picker, panel, precision=HIGH)), "row"
    )
    chol = jnp.linalg.cholesky(gram)
    ortho = jax.scipy.linalg.solve_triangular(chol, panel.T, lower=True).T
    top_ortho = jax.scipy.linalg.solve_triangular(chol, top.T, lower=True).T
    unit_lower, upper = unit_lower_upper(jnp.eye(B, dtype=block.dtype) - top_ortho)
    kernel = jnp.where(live, picker.T - ortho, 0.0)
    basis_rows = jax.scipy.linalg.solve_triangular(upper.T, kernel.T, lower=True).T
    factor = jax.scipy.linalg.solve_triangular(
        unit_lower, upper.T, lower=True, unit_diagonal=True
    ).T
    gathered = lax.all_gather(basis_rows, "row", axis=0, tiled=True)
    basis_cols = lax.dynamic_slice_in_dim(gathered, col_place * col_count, col_count, 0)
    product_cols = lax.psum(jnp.dot(block.T, basis_rows, precision=HIGH), "row")
    product_rows = lax.psum(jnp.dot(block, basis_cols, precision=HIGH), "col")
    image_rows = jnp.dot(product_rows, factor, precision=HIGH)
    image_cols = jnp.dot(product_cols, factor, precision=HIGH)
    inner = lax.psum(jnp.dot(basis_rows.T, image_rows, precision=HIGH), "row")
    coupling = jnp.dot(factor.T, inner, precision=HIGH)
    half_rows = image_rows - 0.5 * jnp.dot(basis_rows, coupling, precision=HIGH)
    half_cols = image_cols - 0.5 * jnp.dot(basis_cols, coupling, precision=HIGH)
    return (
        block
        - jnp.dot(half_rows, basis_cols.T, precision=HIGH)
        - jnp.dot(basis_rows, half_cols.T, precision=HIGH)
    )


def local(matrix):
    current = matrix
    for panel_index in range(PANELS):
        current = panel_update(current, panel_index * B)
    return current


def solution(mesh):
    in_specs = (P("row", "col"),)
    out_specs = P("row", "col")
    return jax.shard_map(local, mesh=mesh, in_specs=in_specs, out_specs=out_specs, check_vma=False)
```

profile of v0, /device:TPU:1, one launch (start us, length us, event | category | flops | bytes accessed | tf_op | source)
XLA Modules:
  0.0 2129.2 jit_solution(11894320768982982306)
XLA Ops:
  8.4 79.0 %all-reduce.11.cloned.1.call-done = f32[256,96]{1,0:T(8,128)} async-done(((f32[256,96]{1,0:T(8,128)}), f32[256,96]{1,0:T(8,128)}) %all-reduce.11.cloned.1.call-update) | async-done | bytes 98320 | tf_op jit(solution)/shard_map/psum | solution.py:15
  91.4 184.5 %all-reduce.25.cloned.1.call-done = (f32[96,96]{0,1:T(8,128)}, f32[96,96]{1,0:T(8,128)}) async-done(((f32[96,96]{0,1:T(8,128)}, f32[96,96]{1,0:T(8,128)}), (f32[96,96]{0,1:T(8,128)}, f32[96,96]{1,0:T(8,128)})) %all-reduce.25.cloned.1.call-update) | async-done | bytes 73744 | tf_op jit(solution)/shard_map/psum | solution.py:45
  277.7 8.8 cholesky.44
  287.8 7.4 custom-call.18
  296.3 150.7 %while.40 = (s32[]{:T(128)}, f32[96,96]{0,1:T(8,128)S(1)}, f32[96,96]{0,1:T(8,128)S(1)}, s32[]{:T(128)}, s32[]{:T(128)}, /*index=5*/s32[]{:T(128)}) while((s32[]{:T(128)}, f32[96,96]{0,1:T(8,128)S(1)}, f32[96,96]{0,1:T(8,128)S(1)}, s32[]{:T(128)}, s32[]{:T(128)}, /*index=5*/s32[]{:T(128)}) %tuple.103), condition=%wide.region_6.9_spmd.clone.clone, body=%wide.region_5.8_spmd.clone.clone.sunk | while | flops 46564 | bytes 152179 | solution.py:31
  447.2 7.4 custom-call.20
  456.8 7.4 custom-call.21
  464.2 3.1 convolution_bitcast_fusion
  467.6 73.9 %all-gather.3.cloned.1.call-done = f32[16384,96]{0,1:T(8,128)} async-done(((f32[256,96]{0,1:T(8,128)}), f32[16384,96]{0,1:T(8,128)}) %all-gather.3.cloned.1.call-update) | async-done | bytes 6291472 | tf_op jit(solution)/shard_map/all_gather | solution.py:57
  541.6 3.8 convolution_bitcast_fusion.1
  545.9 193.1 %all-reduce.15.cloned.1.call-done = f32[2048,96]{0,1:T(8,128)} async-done(((f32[2048,96]{0,1:T(8,128)}), f32[2048,96]{0,1:T(8,128)}) %all-reduce.15.cloned.1.call-update) | async-done | bytes 786448 | tf_op jit(solution)/shard_map/psum | solution.py:59
  739.0 2.9 fusion.102
  742.0 71.0 %all-reduce.13.cloned.1.call-done = f32[256,96]{0,1:T(8,128)} async-done(((f32[256,96]{0,1:T(8,128)}), f32[256,96]{0,1:T(8,128)}) %all-reduce.13.cloned.1.call-update) | async-done | bytes 98320 | tf_op jit(solution)/shard_map/psum | solution.py:60
  814.3 247.2 %psum.88 = f32[96,96]{1,0:T(8,128)S(1)} all-reduce(f32[96,96]{1,0:T(8,128)S(1)} %fusion.100), channel_id=1, replica_groups=mesh['row'=64,'col'=8] {'row'}, use_global_device_ids=true, to_apply=%region_8.13 | all-reduce | flops 9216 | bytes 73728 | tf_op jit(solution)/shard_map/psum | solution.py:63
  1062.0 3.0 fusion.7
  1065.0 3.0 convolution_subtract_fusion.3
  1070.8 67.6 %all-reduce.17.cloned.1.call-done = f32[256,96]{1,0:T(8,128)} async-done(((f32[256,96]{1,0:T(8,128)}), f32[256,96]{1,0:T(8,128)}) %all-reduce.17.cloned.1.call-update) | async-done | bytes 98320 | tf_op jit(solution)/shard_map/psum | solution.py:15
  1142.8 184.3 %all-reduce.23.cloned.1.call-done = (f32[96,96]{0,1:T(8,128)}, f32[96,96]{1,0:T(8,128)}) async-done(((f32[96,96]{0,1:T(8,128)}, f32[96,96]{1,0:T(8,128)}), (f32[96,96]{0,1:T(8,128)}, f32[96,96]{1,0:T(8,128)})) %all-reduce.23.cloned.1.call-update) | async-done | bytes 73744 | tf_op jit(solution)/shard_map/psum | solution.py:45
  1328.8 8.8 cholesky.55
  1338.9 7.4 custom-call.22
  1347.4 150.7 %while.41 = (s32[]{:T(128)}, f32[96,96]{0,1:T(8,128)S(1)}, f32[96,96]{0,1:T(8,128)S(1)}, s32[]{:T(128)}, s32[]{:T(128)}, /*index=5*/s32[]{:T(128)}) while((s32[]{:T(128)}, f32[96,96]{0,1:T(8,128)S(1)}, f32[96,96]{0,1:T(8,128)S(1)}, s32[]{:T(128)}, s32[]{:T(128)}, /*index=5*/s32[]{:T(128)}) %tuple.106), condition=%wide.region_14.19_spmd.clone.clone, body=%wide.region_13.18_spmd.clone.clone.sunk | while | flops 46564 | bytes 152179 | solution.py:31
  1498.3 7.4 custom-call.24
  1507.1 7.4 custom-call.25
  1514.4 5.3 fusion.106
  1520.3 71.5 %all-gather.5.cloned.1.call-done = f32[16384,96]{0,1:T(8,128)} async-done(((f32[256,96]{0,1:T(8,128)}), f32[16384,96]{0,1:T(8,128)}) %all-gather.5.cloned.1.call-update) | async-done | bytes 6291472 | tf_op jit(solution)/shard_map/all_gather | solution.py:57
  1591.8 3.6 fusion.16
  1595.4 195.1 %all-reduce.21.cloned.1.call-done = f32[2048,96]{1,0:T(8,128)} async-done(((f32[2048,96]{1,0:T(8,128)}), f32[2048,96]{1,0:T(8,128)}) %all-reduce.21.cloned.1.call-update) | async-done | bytes 786448 | tf_op jit(solution)/shard_map/psum | solution.py:59
  1792.7 71.0 %all-reduce.19.cloned.1.call-done = f32[256,96]{1,0:T(8,128)} async-done(((f32[256,96]{1,0:T(8,128)}), f32[256,96]{1,0:T(8,128)}) %all-reduce.19.cloned.1.call-update) | async-done | bytes 98320 | tf_op jit(solution)/shard_map/psum | solution.py:60
  1865.1 247.2 %psum.94 = f32[96,96]{1,0:T(8,128)S(1)} all-reduce(f32[96,96]{1,0:T(8,128)S(1)} %fusion.104), channel_id=1, replica_groups=mesh['row'=64,'col'=8] {'row'}, use_global_device_ids=true, to_apply=%region_16.21 | all-reduce | flops 9216 | bytes 73728 | tf_op jit(solution)/shard_map/psum | solution.py:63
  2112.8 3.0 fusion.6
  2115.8 3.0 convolution_subtract_fusion.1
  2118.8 3.3 convolution_subtract_fusion
  (1036 shorter events, 324.2 us)
Async XLA Ops:
  6.5 457.7 %copy-start = (f32[256,2048]{1,0:T(8,128)S(1)}, f32[256,2048]{1,0:T(8,128)}, u32[]{:S(2)}) copy-start(f32[256,2048]{1,0:T(8,128)} %param.12) | copy-start | bytes 6291460
  6.5 80.8 %all-reduce.11.cloned.1.call-start = ((), (), s32[]{:S(2)}) async-start(), calls=%async_computation | async-start | bytes 262144 | tf_op jit(solution)/shard_map/psum | solution.py:15
  8.3 267.7 %all-reduce.25.cloned.1.call-start = ((), (), s32[]{:S(2)}) async-start(), calls=%async_computation.9 | async-start | bytes 196608 | tf_op jit(solution)/shard_map/psum | solution.py:45
  91.4 450.2 %all-gather.3.cloned.1.call-start = ((), (), s32[]{:S(2)}) async-start(), calls=%async_computation.1 | async-start | bytes 6389760 | tf_op jit(solution)/shard_map/all_gather | solution.py:57
  456.8 282.3 %all-reduce.15.cloned.1.call-start = ((), (), s32[]{:S(2)}) async-start(), calls=%async_computation.3 | async-start | bytes 1572864 | tf_op jit(solution)/shard_map/psum | solution.py:59
  467.3 345.6 %all-reduce.13.cloned.1.call-start = ((), (), s32[]{:S(2)}) async-start(), calls=%async_computation.2 | async-start | bytes 196608 | tf_op jit(solution)/shard_map/psum | solution.py:60
  467.6 346.4 %copy-start.1 = (f32[96,256]{1,0:T(8,128)S(1)}, f32[96,256]{1,0:T(8,128)}, u32[]{:S(2)}) copy-start(f32[96,256]{1,0:T(8,128)} %fusion.64) | copy-start | bytes 294916
  545.4 593.1 %all-reduce.17.cloned.1.call-start = ((), (), s32[]{:S(2)}) async-start(), calls=%async_computation.4 | async-start | bytes 262144 | tf_op jit(solution)/shard_map/psum | solution.py:15
  1070.8 256.3 %all-reduce.23.cloned.1.call-start = ((), (), s32[]{:S(2)}) async-start(), calls=%async_computation.8 | async-start | bytes 196608 | tf_op jit(solution)/shard_map/psum | solution.py:45
  1138.5 367.2 %copy-start.3 = (f32[256,96]{1,0:T(8,128)S(1)}, f32[256,96]{1,0:T(8,128)}, u32[]{:S(2)}) copy-start(f32[256,96]{1,0:T(8,128)} %all-reduce.17.cloned.1.call-done) | copy-start | bytes 294916
  1142.5 449.3 %all-gather.5.cloned.1.call-start = ((), (), s32[]{:S(2)}) async-start(), calls=%async_computation.5 | async-start | bytes 6389760 | tf_op jit(solution)/shard_map/all_gather | solution.py:57
  1507.0 283.5 %all-reduce.21.cloned.1.call-start = ((), (), s32[]{:S(2)}) async-start(), calls=%async_computation.7 | async-start | bytes 2097152 | tf_op jit(solution)/shard_map/psum | solution.py:59
  1519.8 344.0 %all-reduce.19.cloned.1.call-start = ((), (), s32[]{:S(2)}) async-start(), calls=%async_computation.6 | async-start | bytes 262144 | tf_op jit(solution)/shard_map/psum | solution.py:60
  1520.3 344.6 %copy-start.2 = (f32[96,256]{1,0:T(8,128)S(1)}, f32[96,256]{1,0:T(8,128)}, u32[]{:S(2)}) copy-start(f32[96,256]{1,0:T(8,128)} %fusion.55) | copy-start | bytes 294916
Sparse Core Ops, SparseCore 0:
  9.7 77.6 all-reduce.10
  91.5 184.4 all-reduce.24
  456.9 84.6 all-gather.2
  545.2 193.7 all-reduce.14
  741.2 71.6 all-reduce.12
  1070.9 67.5 all-reduce.16
  1142.6 184.4 all-reduce.22
  1507.1 84.6 all-gather.4
  1595.2 195.2 all-reduce.20
  1792.8 70.8 all-reduce.18
where the time goes:
time: 2140 us; the launch traced here: 2130 us
  waiting for transfers between devices  1190 us (56%)
  blocking collectives  494 us (23%)
  other arithmetic  214 us (10%)
  local copies, waits for them, and re-layouts  149 us (7%)
  matrix products  55.9 us (3%)
    psum x2, blocking collectives, panel_update(): inner = lax.psum(jnp.dot(basis_rows.T, image_rows, precision=HIGH), 'row')  494 us
    psum x2, waiting for transfers between devices, panel_update(): product_cols = lax.psum(jnp.dot(block.T, basis_rows, precision=HIGH), 'row')  388 us
    psum x2, waiting for transfers between devices, panel_update(): lax.psum((jnp.dot(panel.T, panel, precision=HIGH), jnp.dot(picker, panel,...  369 us
    psum x2, waiting for transfers between devices, broadcast(): return lax.psum(kept, axis)  147 us
    all_gather x2, waiting for transfers between devices, panel_update(): gathered = lax.all_gather(basis_rows, 'row', axis=0, tiled=True)  145 us
    psum x2, waiting for transfers between devices, panel_update(): product_rows = lax.psum(jnp.dot(block, basis_cols, precision=HIGH), 'col')  142 us
    mul x192, other arithmetic, step(): work = work - ratio[:, None] * pivot_row[None, :]  126 us
    dynamic_slice x192, local copies, waits for them, and re-layouts, step(): ratio = jnp.where(index > k, column / pivot_row[k], 0.0)  113 us
  transfers between devices with their start and end apart: 10, of which 10 were waited for; matrix products, arithmetic and copies ran while one was open for 2% of the time, Pallas kernels for 0%

commit v1 on v0

v1 whole, which is shorter than its diff:
```python
import jax
import jax.numpy as jnp
from jax import lax
from jax.experimental import pallas as pl
from jax.experimental.pallas import tpu as pltpu
from jax.sharding import PartitionSpec as P

B = 96
ROWS = 256
COLS = 2048
NX, NZ, NY = 4, 8, 8
F32 = jnp.float32
HIGH = lax.Precision.HIGHEST
MESH = pl.DeviceIdType.MESH

SEND_SEMS = 320


def nn(a, b):
    return lax.dot_general(a, b, (((1,), (0,)), ((), ())), precision=HIGH, preferred_element_type=F32)


def nt(a, b):
    return lax.dot_general(a, b, (((1,), (1,)), ((), ())), precision=HIGH, preferred_element_type=F32)


class Links:
    def __init__(self, send, recv):
        self.send, self.recv, self.count, self.open = send, recv, 0, []
        row, self.y = lax.axis_index("row"), lax.axis_index("col")
        self.row = row
        self.x, self.z, self.k = row // 16, (row // 2) % 8, row % 2

    def sems(self, n):
        first = self.count
        self.count += n
        return first

    def at(self, kind, j):
        x, z, k, y = self.x, self.z, self.k, self.y
        if kind == "x":
            x = (x + j) % NX
        elif kind == "z":
            z = (z + j) % NZ
        elif kind == "k":
            k = (k + j) % 2
        else:
            y = (y + j) % NY
        return (x * 16 + z * 2 + k, y)

    def copy(self, src, dst, sem, kind, j):
        return pltpu.make_async_remote_copy(
            src_ref=src, dst_ref=dst, send_sem=self.send.at[sem], recv_sem=self.recv.at[sem],
            device_id=self.at(kind, j), device_id_type=MESH)

    def finish(self):
        for copy in self.open:
            copy.wait_send()


SIZE = {"x": NX, "z": NZ, "y": NY, "k": 2}


def exchange(links, kind, src_of, dst_of):
    n = SIZE[kind]
    first = links.sems(n)
    copies = []
    for j in range(1, n):
        copy = links.copy(src_of(j), dst_of(j), first + j, kind, j)
        copy.start()
        copies.append(copy)
    links.open += copies
    return copies


def arrive(copies):
    for copy in copies:
        copy.wait_recv()


def place(links, kind, j):
    return (getattr(links, kind) + j) % SIZE[kind]


def ypiece(j):
    return pl.ds(pl.multiple_of(24 * (j // 2), 8), 24), pl.ds(pl.multiple_of(128 * (j % 2), 128), 128)


def zpiece(j):
    return ypiece_rows(j), pl.ds(pl.multiple_of(128 * (j // 2), 128), 128)


def ypiece_rows(j):
    return pl.ds(pl.multiple_of(24 * (j % 2), 8), 24)


def zregion(links):
    return (pl.ds(pl.multiple_of(48 * links.k + 24 * (links.z % 2), 8), 24),
            pl.ds(pl.multiple_of(512 * links.x + 128 * (links.z // 2), 128), 128))


def xregion(links):
    return (pl.ds(pl.multiple_of(48 * links.k, 8), 48),
            pl.ds(pl.multiple_of(512 * links.x, 128), 512))


def kregion(links):
    return pl.ds(pl.multiple_of(48 * links.k, 8), 48), slice(None)


def gather_stage(links, kind, ref, region):
    view = ref.at[region]
    return exchange(links, kind, lambda j: view, lambda j: view)


def ysum_start(links, src, buf):
    return exchange(links, "y",
                    lambda j: src.at[(slice(None),) + ypiece(place(links, "y", j))],
                    lambda j: buf.at[j])


def ysum_mid(links, copies, src, buf, res):
    mine = (slice(None),) + ypiece(links.y)
    arrive(copies)
    total = src[mine]
    for j in range(1, NY):
        total = total + buf[j]
    res[mine] = total
    return gather_stage(links, "y", res, mine)


def psum_core(links, part, bufk):
    rows = pl.ds(pl.multiple_of(48 * (1 - links.k), 8), 48)
    return exchange(links, "k", lambda j: part.at[rows, :], lambda j: bufk)


def psum_x(links, copies, part, bufk, sumk, bufx):
    arrive(copies)
    rows = pl.ds(pl.multiple_of(48 * links.k, 8), 48)
    sumk[...] = part[rows, :] + bufk[...]
    return exchange(links, "x",
                    lambda j: sumk.at[:, pl.ds(pl.multiple_of(512 * place(links, "x", j), 128), 512)],
                    lambda j: bufx.at[j])


def psum_z(links, copies, sumk, bufx, sumx, bufz):
    arrive(copies)
    total = sumk[:, pl.ds(pl.multiple_of(512 * links.x, 128), 512)]
    for j in range(1, NX):
        total = total + bufx[j]
    sumx[...] = total
    return exchange(links, "z", lambda j: sumx.at[zpiece(place(links, "z", j))], lambda j: bufz.at[j])


def psum_back_z(links, copies, sumx, bufz, out):
    arrive(copies)
    total = sumx[zpiece(links.z)]
    for j in range(1, NZ):
        total = total + bufz[j]
    region = zregion(links)
    out[region] = total
    return gather_stage(links, "z", out, region)


def factor_block(b, carry):
    w, v, e, low = carry
    row = lax.broadcasted_iota(jnp.int32, (B, 128), 0)
    lane = lax.broadcasted_iota(jnp.int32, (B, 128), 1)
    alive = row < B - 8 * b
    for s in range(8):
        d = w[s:s + 1, s:s + 1]
        rs = lax.rsqrt(d)
        rs = rs * (1.5 - 0.5 * d * rs * rs)
        rs = rs * (1.5 - 0.5 * d * rs * rs)
        col = jnp.where(alive & (row >= s), jnp.broadcast_to(w[:, s:s + 1], (B, 128)) * rs, 0.0)
        below = jnp.where(row > s, col, 0.0)
        w = w - below * (w[s:s + 1, :] * rs)
        low = jnp.where(lane == s, col, low)
        erow = e[s:s + 1, :] * rs
        e = jnp.where(row == s, jnp.broadcast_to(erow, (B, 128)), e - below * erow)
        vcol = jnp.broadcast_to(v[:, s:s + 1], (B, 128)) + col
        ip = 1.0 / vcol[s:s + 1, :]
        vrow = jnp.where(lane[0:1] == s, -1.0, v[s:s + 1, :]) * ip
        v = jnp.where((lane == s) | (row == s), 0.0, v) - jnp.where(row == s, 1.0, vcol) * vrow

    def turn(m):
        m = pltpu.roll(m, 120, axis=1)
        return jnp.concatenate([m[8:], m[:8]], axis=0)

    e = jnp.concatenate([e[8:], e[:8]], axis=0)
    return turn(w), turn(v), e, turn(low)


def factor(gram, top):
    row = lax.broadcasted_iota(jnp.int32, (B, 128), 0)
    lane = lax.broadcasted_iota(jnp.int32, (B, 128), 1)
    w, v, e, low = lax.fori_loop(
        0, B // 8, factor_block,
        (gram, -top, (row == lane).astype(F32), jnp.zeros((B, 128), F32)))
    return pltpu.roll(low, 96, axis=1), e, pltpu.roll(v, 96, axis=1)


def body(a_ref, o_ref, wsrc, wr, wc, stgk, stgx,
         part, bufk, sumk, bufx, sumx, bufz, yc,
         ysrc, ybuf, yres, csrc, cbuf, cres, pcs, prs, aec, aer, yy, kc, hc, sq, send, recv):
    links = Links(send, recv)
    x, z, k, y, row = links.x, links.z, links.k, links.y, links.row

    barrier = pltpu.get_barrier_semaphore()
    for kind in ("y", "x", "z", "k"):
        for j in range(1, SIZE[kind]):
            pl.semaphore_signal(barrier, inc=1, device_id=links.at(kind, j), device_id_type=MESH)
    pl.semaphore_wait(barrier, NY - 1 + NX - 1 + NZ - 1 + 1)

    lo, hi = (pl.ds(0, 1), pl.ds(1, 2))

    first = links.sems(2 * NY)

    def yscatter(j, part_, sem):
        piece = (part_,) + ypiece(j)
        return links.copy(wsrc.at[piece], wr.at[piece], first + sem, "y", j)

    @pl.when(y == 0)
    def _():
        for g in range(3):
            wsrc[g] = a_ref[:, 0:384].T[g * B:(g + 1) * B]
        wr[(slice(None),) + ypiece(0)] = wsrc[(slice(None),) + ypiece(0)]
        for j in range(1, NY):
            yscatter(j, lo, j).start()
        for j in range(1, NY):
            yscatter(j, hi, NY + j).start()

    core = links.sems(3)
    core_copies = [links.copy(a_ref.at[pl.ds(48, 48), :], stgk.at[0], core, "k", 1),
                   links.copy(a_ref.at[pl.ds(144, 48), :], stgk.at[1], core + 1, "k", 1),
                   links.copy(a_ref.at[pl.ds(240, 16), :], stgk.at[2, pl.ds(0, 16), :], core + 2, "k", 1)]

    @pl.when(row == 0)
    def _():
        for copy in core_copies:
            copy.start()
        stgk[0] = a_ref[0:48, :]
        stgk[1] = a_ref[96:144, :]
        stgk[2] = a_ref[192:240, :]

    @pl.when(row == 1)
    def _():
        stgk[2, 16:48, :] = a_ref[0:32, :]

    xs = links.sems(2 * NX)

    def xscatter(j, part_, sem):
        return links.copy(stgk.at[part_, :, pl.ds(512 * j, 512)], stgx.at[part_], xs + sem, "x", j)

    @pl.when((x == 0) & (z == 0))
    def _():
        for part_, base in ((lo, 0), (hi, NX)):
            @pl.when(k == 1)
            def _():
                for copy in (core_copies[:1] if base == 0 else core_copies[1:]):
                    copy.wait_recv()
            for j in range(1, NX):
                xscatter(j, part_, base + j).start()
        stgx[...] = stgk[:, :, 0:512]

    mine = ypiece(y)

    @pl.when(y != 0)
    def _():
        for g, part_ in enumerate((lo, hi)):
            piece = (part_,) + mine
            links.copy(wr.at[piece], wr.at[piece], first + g * NY + y, "y", 0).wait_recv()

    wr_lo = gather_stage(links, "y", wr, (lo,) + mine)
    wr_hi = gather_stage(links, "y", wr, (hi,) + mine)

    zs = links.sems(2 * NZ)

    def zscatter(j, part_, sem):
        rows, lanes = zpiece(j)
        to_rows = pl.ds(pl.multiple_of(48 * k + 24 * (j % 2), 8), 24)
        to_lanes = pl.ds(pl.multiple_of(512 * x + 128 * (j // 2), 128), 128)
        return links.copy(stgx.at[part_, rows, lanes], wc.at[part_, to_rows, to_lanes], zs + sem, "z", j)

    @pl.when(z == 0)
    def _():
        for part_, base in ((lo, 0), (hi, NX)):
            @pl.when(x != 0)
            def _():
                links.copy(stgx.at[part_], stgx.at[part_], xs + base + x, "x", 0).wait_recv()
            for j in range(1, NZ):
                zscatter(j, part_, (0 if base == 0 else NZ) + j).start()
        wc[(slice(None),) + zregion(links)] = stgx[(slice(None),) + zpiece(0)]

    arrive(wr_lo)

    gl_r = row * ROWS + lax.broadcasted_iota(jnp.int32, (B, ROWS), 1)
    gl_c = y * COLS + lax.broadcasted_iota(jnp.int32, (B, COLS), 1)
    lane128 = lax.broadcasted_iota(jnp.int32, (B, 128), 1)

    def product_cols(pr, mat, out):
        def step(i, _):
            lanes = pl.ds(pl.multiple_of(512 * i, 512), 512)
            out[:, lanes] = nn(pr, mat[:, lanes])
            return 0
        lax.fori_loop(0, 4, step, 0)

    def product_rows(pc, mat):
        def step(i, acc):
            lanes = pl.ds(pl.multiple_of(512 * i, 512), 512)
            return acc + nt(pc[:, lanes], mat[:, lanes])
        return lax.fori_loop(0, 4, step, jnp.zeros((B, ROWS), F32))

    def gram_of(pc, other):
        def step(i, acc):
            lanes = pl.ds(pl.multiple_of(512 * i, 512), 512)
            return acc + nt(pc[:, lanes], other[:, lanes])
        return lax.fori_loop(0, 4, step, jnp.zeros((B, B), F32))

    def widen(m):
        sq[...] = jnp.zeros((B, 128), F32)
        sq[:, 0:B] = m
        return sq[...]

    first_col = y == 0

    def unit_part(chol, trail, width):
        wide = jnp.concatenate([chol] + [jnp.zeros((B, 128), F32)] * (width // 128 - 1), axis=1)
        return pltpu.roll(wide, trail, axis=1)

    pr = jnp.where(gl_r >= B, wr[0], 0.0)
    prs[0] = pr
    product_cols(pr, a_ref, part.at[0])
    ps = psum_core(links, part.at[0], bufk.at[0])

    @pl.when(z != 0)
    def _():
        for g, part_ in enumerate((lo, hi)):
            region = (part_,) + zregion(links)
            links.copy(wc.at[region], wc.at[region], zs + g * NZ + z, "z", 0).wait_recv()

    wlo = gather_stage(links, "z", wc, (lo,) + zregion(links))
    whi = gather_stage(links, "z", wc, (hi,) + zregion(links))
    ps = psum_x(links, ps, part.at[0], bufk.at[0], sumk.at[0], bufx.at[0])
    arrive(wlo)
    wlo = gather_stage(links, "x", wc, (lo,) + xregion(links))
    ps = psum_z(links, ps, sumk.at[0], bufx.at[0], sumx.at[0], bufz.at[0])
    arrive(wlo)
    wlo = gather_stage(links, "k", wc, (lo,) + kregion(links))
    arrive(whi)
    whi = gather_stage(links, "x", wc, (hi,) + xregion(links))
    arrive(wlo)

    pcs[0] = jnp.where(gl_c >= B, wc[0], 0.0)

    def panel(p, ps, mat, wc_p, wr_p, whi):
        trail = (p + 1) * B
        pc = pcs.at[p]
        ysrc[p, 0, :, 0:128] = widen(gram_of(pc, pc))
        ysrc[p, 0, :, 128:256] = jnp.where(first_col, pc[:, 0:128], 0.0)
        ysrc[p, 1] = jnp.where(first_col, pc[:, 128:384], 0.0)
        ysrc[p, 2] = product_rows(pc, mat)
        ys = ysum_start(links, ysrc.at[p], ybuf.at[p])
        ps = psum_back_z(links, ps, sumx.at[p], bufz.at[p], yc.at[p])
        ys = ysum_mid(links, ys, ysrc.at[p], ybuf.at[p], yres.at[p])
        arrive(ps)
        ps = gather_stage(links, "x", yc.at[p], xregion(links))
        if whi is not None:
            arrive(whi)
            whi = gather_stage(links, "k", wc, (hi,) + kregion(links))
        arrive(ys)
        gram = yres[p, 0, :, 0:128]
        pwin = jnp.concatenate([yres[p, 0, :, 128:256], yres[p, 1]], axis=1)
        top = jnp.where(lane128 < B, pltpu.roll(pwin, 384 - trail, axis=1)[:, 0:128], 0.0)
        chol, chol_inv, v = factor(gram, top)
        arrive(ps)
        ps = gather_stage(links, "k", yc.at[p], kregion(links))
        nt_ = nn(v.T[0:B], chol_inv)[:, 0:B]
        low = chol[:, 0:B]
        unit = unit_part(chol, trail, 512)
        kc[...] = -pc[...]
        kc[:, 0:512] = kc[:, 0:512] + jnp.where(first_col, unit, 0.0)
        arrive(ps)
        if whi is not None:
            arrive(whi)

        def make_y(i, _):
            lanes = pl.ds(pl.multiple_of(512 * i, 512), 512)
            yy[:, lanes] = nn(low, wc_p[:, lanes]) - yc[p, :, lanes]
            return 0
        lax.fori_loop(0, 4, make_y, 0)
        csrc[p, 0, :, 0:128] = widen(gram_of(kc, yy))
        csrc[p, 0, :, 128:256] = jnp.where(first_col, yy[:, 0:128], 0.0)
        csrc[p, 1] = jnp.where(first_col, yy[:, 128:384], 0.0)
        cs = ysum_start(links, csrc.at[p], cbuf.at[p])
        kr = (jnp.where(row == 0, unit[:, 0:256], 0.0) + jnp.where(row == 1, unit[:, 256:512], 0.0)) - prs[p]
        yr = nn(low, wr_p[...]) - yres[p, 2]
        nty = nn(nt_, yr)
        cs = ysum_mid(links, cs, csrc.at[p], cbuf.at[p], cres.at[p])
        arrive(cs)
        c = cres[p, 0, :, 0:B]
        nd = -0.5 * nt(nn(nt_, c), nt_)
        hr = nty + nn(nd, kr)

        def make_h(i, _):
            lanes = pl.ds(pl.multiple_of(512 * i, 512), 512)
            hc[:, lanes] = nn(nt_, yy[:, lanes]) + nn(nd, kc[:, lanes])
            return 0
        lax.fori_loop(0, 4, make_h, 0)
        left = jnp.concatenate([hr, kr], axis=0).T

        def update(i, _):
            lanes = pl.ds(pl.multiple_of(512 * i, 512), 512)
            right = jnp.concatenate([kc[:, lanes], hc[:, lanes]], axis=0)
            o_ref[:, lanes] = mat[:, lanes] - nn(left, right)
            return 0

        if p == 1:
            lax.fori_loop(0, 4, update, 0)
            return None

        ywin = jnp.concatenate([cres[p, 0, :, 128:256], cres[p, 1]], axis=1)
        kwin = unit[:, 0:384] - pwin
        hwin = nn(nt_, ywin) + nn(nd, kwin)
        rows = jnp.concatenate([hwin, kwin], axis=0).T[B:3 * B]
        new = nn(rows, jnp.concatenate([kr, hr], axis=0))
        prs[1] = jnp.where(gl_r >= 2 * B, wr[1] - new[0:B], 0.0)
        aer[...] = wr[2] - new[B:]

        def next_rows(i, _):
            lanes = pl.ds(pl.multiple_of(512 * i, 512), 512)
            right = jnp.concatenate([kc[:, lanes], hc[:, lanes]], axis=0)
            fresh = nn(rows, right)
            pcs[1, :, lanes] = wc[1, :, lanes] - fresh[0:B]
            aec[:, lanes] = wc[2, :, lanes] - fresh[B:]
            return 0

        lax.fori_loop(0, 4, update, 0)
        product_cols(prs[1], o_ref, part.at[1])
        ps = psum_core(links, part.at[1], bufk.at[1])
        lax.fori_loop(0, 4, next_rows, 0)
        pcs[1] = jnp.where(gl_c >= 2 * B, pcs[1], 0.0)
        ps = psum_x(links, ps, part.at[1], bufk.at[1], sumk.at[1], bufx.at[1])
        return psum_z(links, ps, sumk.at[1], bufx.at[1], sumx.at[1], bufz.at[1])

    arrive(wr_hi)
    ps = panel(0, ps, a_ref, wc.at[1], wr.at[1], whi)
    panel(1, ps, o_ref, aec, aer, None)

    @pl.when(y == 0)
    def _():
        for j in range(1, NY):
            yscatter(j, lo, j).wait_send()
            yscatter(j, hi, NY + j).wait_send()

    @pl.when(row == 0)
    def _():
        for copy in core_copies:
            copy.wait_send()

    @pl.when((x == 0) & (z == 0))
    def _():
        for j in range(1, NX):
            xscatter(j, lo, j).wait_send()
            xscatter(j, hi, NX + j).wait_send()

    @pl.when(z == 0)
    def _():
        for j in range(1, NZ):
            zscatter(j, lo, j).wait_send()
            zscatter(j, hi, NZ + j).wait_send()

    links.finish()


def local(matrix):
    vmem = pltpu.VMEM
    return pl.pallas_call(
        body,
        out_shape=jax.ShapeDtypeStruct((ROWS, COLS), F32),
        in_specs=[pl.BlockSpec(memory_space=pltpu.VMEM)],
        out_specs=pl.BlockSpec(memory_space=pltpu.VMEM),
        scratch_shapes=[
            vmem((3, B, ROWS), F32), vmem((3, B, ROWS), F32), vmem((3, B, COLS), F32),
            vmem((3, 48, COLS), F32), vmem((3, 48, 512), F32),
            vmem((2, B, COLS), F32), vmem((2, 48, COLS), F32), vmem((2, 48, COLS), F32),
            vmem((2, NX, 48, 512), F32), vmem((2, 48, 512), F32), vmem((2, NZ, 24, 128), F32), vmem((2, B, COLS), F32),
            vmem((2, 3, B, 256), F32), vmem((2, NY, 3, 24, 128), F32), vmem((2, 3, B, 256), F32),
            vmem((2, 2, B, 256), F32), vmem((2, NY, 2, 24, 128), F32), vmem((2, 2, B, 256), F32),
            vmem((2, B, COLS), F32), vmem((2, B, ROWS), F32), vmem((B, COLS), F32), vmem((B, ROWS), F32),
            vmem((B, COLS), F32), vmem((B, COLS), F32), vmem((B, COLS), F32), vmem((B, 128), F32),
            pltpu.SemaphoreType.DMA((SEND_SEMS,)), pltpu.SemaphoreType.DMA((SEND_SEMS,)),
        ],
        compiler_params=pltpu.CompilerParams(
            collective_id=0, has_side_effects=True, vmem_limit_bytes=56 * 1024 * 1024),
        name="two_panels",
    )(matrix)


def solution(mesh):
    return jax.shard_map(local, mesh=mesh, in_specs=(P("row", "col"),), out_specs=P("row", "col"), check_vma=False)
```

time: 2140 us -> 188 us (0.09)
  waiting for transfers between devices: 1190 us -> 0 us
  blocking collectives: 494 us -> 0 us
  other arithmetic: 214 us -> 0 us
  Pallas kernels: 0 us -> 183 us
  local copies, waits for them, and re-layouts: 149 us -> 3.14 us
  matrix products: 55.9 us -> 0 us
    psum x8 -> x0, waiting for transfers between devices: 1050 us -> none  [the longest x2 388 us: panel_update(): product_cols = lax.psum(jnp.dot(block.T, basis_rows, precision=HIGH), 'row')]
    psum x2 -> x0, blocking collectives: 494 us -> none  [panel_update(): inner = lax.psum(jnp.dot(basis_rows.T, image_rows, precision=HIGH), 'row')]
    pallas_call x0 -> x1, Pallas kernels: none -> 183 us  [local(): pl.pallas_call(body, out_shape=jax.ShapeDtypeStruct((ROWS, COLS), F32), i...]
    dynamic_slice x384 -> x0, local copies, waits for them, and re-layouts: 147 us -> none  [the longest x192 113 us: step(): ratio = jnp.where(index > k, column / pivot_row[k], 0.0)]
    all_gather x2 -> x0, waiting for transfers between devices: 145 us -> none  [panel_update(): gathered = lax.all_gather(basis_rows, 'row', axis=0, tiled=True)]
    mul x192 -> x0, other arithmetic: 126 us -> none  [step(): work = work - ratio[:, None] * pivot_row[None, :]]
    another operation x16 -> x0, other arithmetic: 64.5 us -> none  [the longest x6 18.9 us: panel_update(): chol = jnp.linalg.cholesky(gram)]
    dot_general x24 -> x0, matrix products: 49.9 us -> none  [the longest x2 8.39 us: panel_update(): product_cols = lax.psum(jnp.dot(block.T, basis_rows, precision=HIGH), 'row')]
  transfers between devices with their start and end apart: 10 -> 0, of which waited for: 10 -> 0; matrix products, arithmetic and copies ran while one was open for 2% -> 0% of each run, Pallas kernels for 0% -> 0%
where the time goes in v1:
time: 188 us; the launch traced here: 187 us
  Pallas kernels  183 us (97%)
  local copies, waits for them, and re-layouts  3.14 us (2%)
    pallas_call x1, Pallas kernels, local(): pl.pallas_call(body, out_shape=jax.ShapeDtypeStruct((ROWS, COLS), F32), i...  183 us

profile of v1, /device:TPU:1, one launch (start us, length us, event | category | flops | bytes accessed | tf_op | source)
XLA Modules:
  0.0 186.6 jit_solution(6953328044916934285)
XLA Ops:
  0.0 183.5 %two_panels.1 = f32[256,2048]{1,0:T(8,128)} custom-call(f32[256,2048]{1,0:T(8,128)} %a_ref.1), custom_call_target="tpu_custom_call" | custom-call | tf_op jit(solution)/shard_map/two_panels/pallas_call | solution.py:478
  183.5 3.1 %copy.3 = f32[256,2048]{1,0:T(8,128)} copy(f32[256,2048]{1,0:T(8,128)} %two_panels.1) | data formatting | bytes 4194304

commit v2 on v1

v2 whole, which is shorter than its diff:
```python
import jax
import jax.numpy as jnp
from jax import lax
from jax.experimental import pallas as pl
from jax.experimental.pallas import tpu as pltpu
from jax.sharding import PartitionSpec as P

B = 96
ROWS = 256
COLS = 2048
NX, NZ, NY = 4, 8, 8
F32 = jnp.float32
HIGH = lax.Precision.HIGHEST
MESH = pl.DeviceIdType.MESH

SEND_SEMS = 320


def nn(a, b):
    return lax.dot_general(a, b, (((1,), (0,)), ((), ())), precision=HIGH, preferred_element_type=F32)


def nt(a, b):
    return lax.dot_general(a, b, (((1,), (1,)), ((), ())), precision=HIGH, preferred_element_type=F32)


class Links:
    def __init__(self, send, recv):
        self.send, self.recv, self.count, self.open = send, recv, 0, []
        row, self.y = lax.axis_index("row"), lax.axis_index("col")
        self.row = row
        self.x, self.z, self.k = row // 16, (row // 2) % 8, row % 2

    def sems(self, n):
        first = self.count
        self.count += n
        return first

    def at(self, kind, j):
        x, z, k, y = self.x, self.z, self.k, self.y
        if kind == "x":
            x = (x + j) % NX
        elif kind == "z":
            z = (z + j) % NZ
        elif kind == "k":
            k = (k + j) % 2
        else:
            y = (y + j) % NY
        return (x * 16 + z * 2 + k, y)

    def copy(self, src, dst, sem, kind, j):
        return pltpu.make_async_remote_copy(
            src_ref=src, dst_ref=dst, send_sem=self.send.at[sem], recv_sem=self.recv.at[sem],
            device_id=self.at(kind, j), device_id_type=MESH)

    def finish(self):
        for copy in self.open:
            copy.wait_send()


SIZE = {"x": NX, "z": NZ, "y": NY, "k": 2}


def exchange(links, kind, src_of, dst_of):
    n = SIZE[kind]
    first = links.sems(n)
    copies = []
    for j in range(1, n):
        copy = links.copy(src_of(j), dst_of(j), first + j, kind, j)
        copy.start()
        copies.append(copy)
    links.open += copies
    return copies


def arrive(copies):
    for copy in copies:
        copy.wait_recv()


def place(links, kind, j):
    return (getattr(links, kind) + j) % SIZE[kind]


def ypiece(j):
    return pl.ds(pl.multiple_of(24 * (j // 2), 8), 24), pl.ds(pl.multiple_of(128 * (j % 2), 128), 128)


def zpiece(j):
    return ypiece_rows(j), pl.ds(pl.multiple_of(128 * (j // 2), 128), 128)


def ypiece_rows(j):
    return pl.ds(pl.multiple_of(24 * (j % 2), 8), 24)


def zregion(links):
    return (pl.ds(pl.multiple_of(48 * links.k + 24 * (links.z % 2), 8), 24),
            pl.ds(pl.multiple_of(512 * links.x + 128 * (links.z // 2), 128), 128))


def xregion(links):
    return (pl.ds(pl.multiple_of(48 * links.k, 8), 48),
            pl.ds(pl.multiple_of(512 * links.x, 128), 512))


def kregion(links):
    return pl.ds(pl.multiple_of(48 * links.k, 8), 48), slice(None)


def gather_stage(links, kind, ref, region):
    view = ref.at[region]
    return exchange(links, kind, lambda j: view, lambda j: view)


def ysum_start(links, src, buf):
    return exchange(links, "y",
                    lambda j: src.at[(slice(None),) + ypiece(place(links, "y", j))],
                    lambda j: buf.at[j])


def ysum_mid(links, copies, src, buf, res):
    mine = (slice(None),) + ypiece(links.y)
    arrive(copies)
    total = src[mine]
    for j in range(1, NY):
        total = total + buf[j]
    res[mine] = total
    return gather_stage(links, "y", res, mine)


def psum_core(links, part, bufk):
    rows = pl.ds(pl.multiple_of(48 * (1 - links.k), 8), 48)
    return exchange(links, "k", lambda j: part.at[rows, :], lambda j: bufk)


def psum_x(links, copies, part, bufk, sumk, bufx):
    arrive(copies)
    rows = pl.ds(pl.multiple_of(48 * links.k, 8), 48)
    sumk[...] = part[rows, :] + bufk[...]
    return exchange(links, "x",
                    lambda j: sumk.at[:, pl.ds(pl.multiple_of(512 * place(links, "x", j), 128), 512)],
                    lambda j: bufx.at[j])


def psum_z(links, copies, sumk, bufx, sumx, bufz):
    arrive(copies)
    total = sumk[:, pl.ds(pl.multiple_of(512 * links.x, 128), 512)]
    for j in range(1, NX):
        total = total + bufx[j]
    sumx[...] = total
    return exchange(links, "z", lambda j: sumx.at[zpiece(place(links, "z", j))], lambda j: bufz.at[j])


def psum_back_z(links, copies, sumx, bufz, out):
    arrive(copies)
    total = sumx[zpiece(links.z)]
    for j in range(1, NZ):
        total = total + bufz[j]
    region = zregion(links)
    out[region] = total
    return gather_stage(links, "z", out, region)


def small_core(links, src, bufk):
    rows = pl.ds(pl.multiple_of(48 * (1 - links.k), 8), 48)
    return exchange(links, "k", lambda j: src.at[rows, :], lambda j: bufk)


def small_x(links, copies, src, bufk, parts):
    arrive(copies)
    parts[links.x] = src[pl.ds(pl.multiple_of(48 * links.k, 8), 48), :] + bufk[...]
    view = parts.at[links.x]
    return exchange(links, "x", lambda j: view, lambda j: view)


def small_z(links, copies, xparts, parts):
    arrive(copies)
    total = xparts[0]
    for j in range(1, NX):
        total = total + xparts[j]
    parts[links.z] = total
    view = parts.at[links.z]
    return exchange(links, "z", lambda j: view, lambda j: view)


def small_back(links, copies, zparts, out):
    arrive(copies)
    total = zparts[0]
    for j in range(1, NZ):
        total = total + zparts[j]
    out[kregion(links)] = total
    return gather_stage(links, "k", out, kregion(links))


def factor_block(b, carry):
    w, v, e, low = carry
    row = lax.broadcasted_iota(jnp.int32, (B, 128), 0)
    lane = lax.broadcasted_iota(jnp.int32, (B, 128), 1)
    lane1 = lane[0:1]
    alive = row < B - 8 * b
    for first in range(0, 8, 4):
        steps = range(first, first + 4)
        wcol = [jnp.broadcast_to(w[:, s:s + 1], (B, 128)) for s in steps]
        vcol = [jnp.broadcast_to(v[:, s:s + 1], (B, 128)) for s in steps]
        wrow = [w[s:s + 1, :] for s in steps]
        vrow = [v[s:s + 1, :] for s in steps]
        erow = [e[s:s + 1, :] for s in steps]
        for i, s in enumerate(steps):
            rs = lax.rsqrt(wcol[i][s:s + 1, :])
            col = jnp.where(alive & (row >= s), wcol[i] * rs, 0.0)
            wr = wrow[i] * rs
            er = erow[i] * rs
            vc = vcol[i] + col
            ip = 1.0 / vc[s:s + 1, :]
            vr = jnp.where(lane1 == s, -1.0, vrow[i]) * ip
            vm = jnp.where(row == s, 1.0, vc)
            for j in range(i + 1, 4):
                t = first + j
                cj = col[t:t + 1, :]
                wcol[j] = wcol[j] - col * cj
                wrow[j] = wrow[j] - cj * wr
                erow[j] = erow[j] - cj * er
                vj = vcol[j][s:s + 1, :] * ip
                vcol[j] = jnp.where(row == s, 0.0, vcol[j]) - vm * vj
                vrow[j] = jnp.where(lane1 == s, 0.0, vrow[j]) - vm[t:t + 1, :] * vr
            w = w - col * wr
            low = jnp.where(lane == s, col, low)
            e = jnp.where(row == s, jnp.broadcast_to(er, (B, 128)), e - jnp.where(row > s, col, 0.0) * er)
            v = jnp.where((lane == s) | (row == s), 0.0, v) - vm * vr

    def turn(m):
        m = pltpu.roll(m, 120, axis=1)
        return jnp.concatenate([m[8:], m[:8]], axis=0)

    e = jnp.concatenate([e[8:], e[:8]], axis=0)
    return turn(w), turn(v), e, turn(low)


def factor_start(gram, top):
    row = lax.broadcasted_iota(jnp.int32, (B, 128), 0)
    lane = lax.broadcasted_iota(jnp.int32, (B, 128), 1)
    return gram, -top, (row == lane).astype(F32), jnp.zeros((B, 128), F32)


def factor_some(first, last, state):
    return lax.fori_loop(first, last, factor_block, state)


def factor_end(state):
    _, v, e, low = state
    low = pltpu.roll(low, 96, axis=1)[:, 0:B]
    v = pltpu.roll(v, 96, axis=1)
    return low, nn(v.T[0:B], e)[:, 0:B]


def body(a_ref, o_ref, wsrc, wr, wc, stgk, stgx,
         part, bufk, sumk, bufx, sumx, bufz, yc,
         gsrc, gbuf, gres, rsrc, rbuf, rres, csrc, cbuf, cres, esrc, ebuf, eres,
         ssrc, sbufk, sx, sz, sres,
         pcs, prs, aec, aer, yy, kc, hc, sq, send, recv):
    links = Links(send, recv)
    x, z, k, y, row = links.x, links.z, links.k, links.y, links.row

    barrier = pltpu.get_barrier_semaphore()
    for kind in ("y", "x", "z", "k"):
        for j in range(1, SIZE[kind]):
            pl.semaphore_signal(barrier, inc=1, device_id=links.at(kind, j), device_id_type=MESH)

    @pl.when(y == 0)
    def _():
        wsrc[0] = a_ref[:, 0:128].T[0:B]

    pl.semaphore_wait(barrier, NY - 1 + NX - 1 + NZ - 1 + 1)

    lo, hi = (pl.ds(0, 1), pl.ds(1, 2))
    origin = (x == 0) & (z == 0)

    ysc = links.sems(2 * NY)
    core = links.sems(3)
    xsc = links.sems(2 * NX)
    zsc = links.sems(2 * NZ)
    mine = ypiece(y)

    def yscatter(j, part_, sem):
        piece = (part_,) + ypiece(j)
        return links.copy(wsrc.at[piece], wr.at[piece], ysc + sem, "y", j)

    core_copies = [links.copy(a_ref.at[pl.ds(48, 48), :], stgk.at[0], core, "k", 1),
                   links.copy(a_ref.at[pl.ds(144, 48), :], stgk.at[1], core + 1, "k", 1),
                   links.copy(a_ref.at[pl.ds(240, 16), :], stgk.at[2, pl.ds(0, 16), :], core + 2, "k", 1)]

    def xscatter(j, part_, sem):
        return links.copy(stgk.at[part_, :, pl.ds(512 * j, 512)], stgx.at[part_], xsc + sem, "x", j)

    def zscatter(j, part_, sem):
        rows, lanes = zpiece(j)
        to_rows = pl.ds(pl.multiple_of(48 * k + 24 * (j % 2), 8), 24)
        to_lanes = pl.ds(pl.multiple_of(512 * x + 128 * (j // 2), 128), 128)
        return links.copy(stgx.at[part_, rows, lanes], wc.at[part_, to_rows, to_lanes], zsc + sem, "z", j)

    def y_out(part_, g):
        @pl.when(y == 0)
        def _():
            wr[(part_,) + ypiece(0)] = wsrc[(part_,) + ypiece(0)]
            for j in range(1, NY):
                yscatter(j, part_, g * NY + j).start()

    def y_in(part_, g):
        piece = (part_,) + mine

        @pl.when(y != 0)
        def _():
            links.copy(wr.at[piece], wr.at[piece], ysc + g * NY + y, "y", 0).wait_recv()

        return gather_stage(links, "y", wr, piece)

    def x_out(part_, g):
        @pl.when(origin)
        def _():
            @pl.when(k == 1)
            def _():
                for copy in (core_copies[:1] if g == 0 else core_copies[1:]):
                    copy.wait_recv()
            for j in range(1, NX):
                xscatter(j, part_, g * NX + j).start()
            stgx[part_] = stgk[part_, :, 0:512]

    def z_out(part_, g):
        @pl.when(z == 0)
        def _():
            @pl.when(x != 0)
            def _():
                links.copy(stgx.at[part_], stgx.at[part_], xsc + g * NX + x, "x", 0).wait_recv()
            for j in range(1, NZ):
                zscatter(j, part_, g * NZ + j).start()
            wc[(part_,) + zregion(links)] = stgx[(part_,) + zpiece(0)]

    def z_in(part_, g):
        region = (part_,) + zregion(links)

        @pl.when(z != 0)
        def _():
            links.copy(wc.at[region], wc.at[region], zsc + g * NZ + z, "z", 0).wait_recv()

        return gather_stage(links, "z", wc, region)

    y_out(lo, 0)

    @pl.when(row == 0)
    def _():
        core_copies[0].start()
        stgk[0] = a_ref[0:48, :]

    x_out(lo, 0)
    wr_lo = y_in(lo, 0)

    @pl.when(row == 0)
    def _():
        for copy in core_copies[1:]:
            copy.start()
        stgk[1] = a_ref[96:144, :]
        stgk[2] = a_ref[192:240, :]

    @pl.when(row == 1)
    def _():
        stgk[2, 16:48, :] = a_ref[0:32, :]

    @pl.when(y == 0)
    def _():
        t = a_ref[:, 0:384].T
        wsrc[1] = t[B:2 * B]
        wsrc[2] = t[2 * B:3 * B]

    z_out(lo, 0)
    y_out(hi, 1)

    gl_r = row * ROWS + lax.broadcasted_iota(jnp.int32, (B, ROWS), 1)
    gl_c = y * COLS + lax.broadcasted_iota(jnp.int32, (B, COLS), 1)
    lane128 = lax.broadcasted_iota(jnp.int32, (B, 128), 1)
    first_col = y == 0

    def chunks(step):
        def run(i, _):
            step(pl.ds(pl.multiple_of(512 * i, 512), 512))
            return 0
        lax.fori_loop(0, 4, run, 0)

    def product_cols(pr, mat, out):
        def step(lanes):
            out[:, lanes] = nn(pr, mat[:, lanes])
        chunks(step)

    def product_rows(pc, mat, width):
        def step(i, acc):
            lanes = pl.ds(pl.multiple_of(512 * i, 512), 512)
            return acc + nt(pc[:, lanes], mat[:, lanes])
        return lax.fori_loop(0, 4, step, jnp.zeros((B, width), F32))

    def widen(m):
        sq[...] = jnp.zeros((B, 128), F32)
        sq[:, 0:B] = m
        return sq[...]

    def square(window, at):
        width = window.shape[1]
        return jnp.where(lane128 < B, pltpu.roll(window, width - at, axis=1)[:, 0:128], 0.0)

    def col_square(ref, at):
        return jnp.where(first_col, square(ref[:, 0:384], at), 0.0)

    def unit_part(chol, trail):
        wide = jnp.concatenate([widen(chol), jnp.zeros((B, 384), F32)], axis=1)
        return pltpu.roll(wide, trail, axis=1)

    def make_k(unit, p):
        kc[...] = -pcs[p]
        kc[:, 0:512] = kc[:, 0:512] + jnp.where(first_col, unit, 0.0)
        return (jnp.where(row == 0, unit[:, 0:256], 0.0) + jnp.where(row == 1, unit[:, 256:512], 0.0)) - prs[p]

    arrive(wr_lo)
    prs[0] = jnp.where(gl_r >= B, wr[0], 0.0)
    product_cols(prs[0], a_ref, part.at[0])
    ps = psum_core(links, part.at[0], bufk.at[0])
    wlo = z_in(lo, 0)
    ps = psum_x(links, ps, part.at[0], bufk.at[0], sumk.at[0], bufx.at[0])
    x_out(hi, 1)
    wr_hi = y_in(hi, 1)
    arrive(wlo)
    wlo = gather_stage(links, "x", wc, (lo,) + xregion(links))
    ps = psum_z(links, ps, sumk.at[0], bufx.at[0], sumx.at[0], bufz.at[0])
    arrive(wlo)
    wlo = gather_stage(links, "k", wc, (lo,) + kregion(links))
    z_out(hi, 1)
    arrive(wlo)
    pcs[0] = jnp.where(gl_c >= B, wc[0], 0.0)
    gsrc[0, 0, :, 0:128] = widen(product_rows(pcs.at[0], pcs.at[0], B))
    gsrc[0, 0, :, 128:256] = col_square(pcs.at[0], B)
    gs = ysum_start(links, gsrc.at[0], gbuf.at[0])
    whi = z_in(hi, 1)
    ps = psum_back_z(links, ps, sumx.at[0], bufz.at[0], yc.at[0])
    rsrc[0, 0] = product_rows(pcs.at[0], a_ref, ROWS)
    gs = ysum_mid(links, gs, gsrc.at[0], gbuf.at[0], gres.at[0])
    rs = ysum_start(links, rsrc.at[0], rbuf.at[0])
    arrive(ps)
    ps = gather_stage(links, "x", yc.at[0], xregion(links))
    arrive(whi)
    whi = gather_stage(links, "x", wc, (hi,) + xregion(links))
    arrive(gs)
    top = gres[0, 0, :, 128:256]
    state = factor_start(gres[0, 0, :, 0:128], top)
    arrive(ps)
    ps = gather_stage(links, "k", yc.at[0], kregion(links))
    state = factor_some(0, 4, state)
    arrive(whi)
    whi = gather_stage(links, "k", wc, (hi,) + kregion(links))
    arrive(ps)
    arrive(whi)
    csrc[0, 0, :, 0:128] = widen(product_rows(pcs.at[0], yc.at[0], B))
    csrc[0, 0, :, 128:256] = col_square(yc.at[0], B)
    csrc[0, 1, :, 0:128] = col_square(wc.at[1], B)
    csrc[0, 1, :, 128:256] = col_square(yc.at[0], 2 * B)
    cs = ysum_start(links, csrc.at[0], cbuf.at[0])
    rs = ysum_mid(links, rs, rsrc.at[0], rbuf.at[0], rres.at[0])
    state = factor_some(4, 8, state)
    cs = ysum_mid(links, cs, csrc.at[0], cbuf.at[0], cres.at[0])
    esrc[0, :, 0:128] = col_square(wc.at[0], 2 * B)
    esrc[0, :, 128:256] = col_square(wc.at[1], 2 * B)
    esrc[1, :, 0:128] = col_square(wc.at[2], 2 * B)
    esrc[1, :, 128:256] = jnp.zeros((B, 128), F32)
    es = ysum_start(links, esrc, ebuf)
    state = factor_some(8, 12, state)
    low, nt_ = factor_end(state)
    unit = unit_part(low, B)
    kr = make_k(unit, 0)

    def image(lanes):
        yy[:, lanes] = nn(low, wc[1, :, lanes]) - yc[0, :, lanes]
    chunks(image)
    arrive(rs)
    arrive(wr_hi)
    yr = nn(low, wr[1]) - rres[0, 0]
    es = ysum_mid(links, es, esrc, ebuf, eres)
    arrive(cs)

    def coupling(low, nt_, att, yt, phi):
        head = nn(low, att) - yt
        c = nt(head, low) - nt(low, yt) + phi
        return head, -0.5 * nt(nn(nt_, c), nt_)

    head, nd = coupling(low, nt_, cres[0, 1, :, 0:B], cres[0, 0, :, 128:128 + B], cres[0, 0, :, 0:B])
    kt = low - top[:, 0:B]
    ht = nn(nt_, head) + nn(nd, kt)
    rows1 = jnp.concatenate([ht, kt], axis=0).T

    def next_panel(lanes):
        hcl = nn(nt_, yy[:, lanes]) + nn(nd, kc[:, lanes])
        hc[:, lanes] = hcl
        fresh = wc[1, :, lanes] - nn(rows1, jnp.concatenate([kc[:, lanes], hcl], axis=0))
        pcs[1, :, lanes] = fresh
    chunks(next_panel)
    pcs[1] = jnp.where(gl_c >= 2 * B, pcs[1], 0.0)
    gsrc[1, 0, :, 0:128] = widen(product_rows(pcs.at[1], pcs.at[1], B))
    gsrc[1, 0, :, 128:256] = col_square(pcs.at[1], 2 * B)
    gs = ysum_start(links, gsrc.at[1], gbuf.at[1])
    hr = nn(nt_, yr) + nn(nd, kr)
    right_r = jnp.concatenate([kr, hr], axis=0)
    prs[1] = jnp.where(gl_r >= 2 * B, wr[1] - nn(rows1, right_r), 0.0)
    left = jnp.concatenate([hr, kr], axis=0).T

    def update(lanes):
        right = jnp.concatenate([kc[:, lanes], hc[:, lanes]], axis=0)
        o_ref[:, lanes] = a_ref[:, lanes] - nn(left, right)
    chunks(update)

    rsrc[1, 0] = product_rows(pcs.at[1], o_ref, ROWS)
    rs = ysum_start(links, rsrc.at[1], rbuf.at[1])
    product_cols(prs[1], o_ref, part.at[1])
    ps = psum_core(links, part.at[1], bufk.at[1])
    gs = ysum_mid(links, gs, gsrc.at[1], gbuf.at[1], gres.at[1])
    ps = psum_x(links, ps, part.at[1], bufk.at[1], sumk.at[1], bufx.at[1])
    arrive(es)
    kt = -eres[0, :, 0:B]
    ht = nn(nt_, nn(low, eres[0, :, 128:128 + B]) - cres[0, 1, :, 128:128 + B]) + nn(nd, kt)
    rows2 = jnp.concatenate([ht, kt], axis=0).T
    att = eres[1, :, 0:B] - nn(rows2, jnp.concatenate([kt, ht], axis=0))
    aer[...] = wr[2] - nn(rows2, right_r)
    rs = ysum_mid(links, rs, rsrc.at[1], rbuf.at[1], rres.at[1])

    def next_rows(lanes):
        aec[:, lanes] = wc[2, :, lanes] - nn(rows2, jnp.concatenate([kc[:, lanes], hc[:, lanes]], axis=0))
    chunks(next_rows)
    ps = psum_z(links, ps, sumk.at[1], bufx.at[1], sumx.at[1], bufz.at[1])
    arrive(gs)
    top = gres[1, 0, :, 128:256]
    state = factor_some(0, 6, factor_start(gres[1, 0, :, 0:128], top))
    arrive(rs)
    yrow = rres[1, 0]
    none = jnp.zeros((B, ROWS), F32)
    ssrc[:, 0:128] = widen(nt(prs[1], yrow))
    ssrc[:, 128:256] = (jnp.where(row == 0, square(jnp.concatenate([yrow, none], axis=1), 2 * B), 0.0)
                        + jnp.where(row == 1, square(jnp.concatenate([none, yrow], axis=1), 2 * B), 0.0))
    ss = small_core(links, ssrc, sbufk)
    state = factor_some(6, 8, state)
    ss = small_x(links, ss, ssrc, sbufk, sx)
    ps = psum_back_z(links, ps, sumx.at[1], bufz.at[1], yc.at[1])
    state = factor_some(8, 12, state)
    ss = small_z(links, ss, sx, sz)
    low, nt_ = factor_end(state)
    kr = make_k(unit_part(low, 2 * B), 1)
    yr = nn(low, aer[...]) - yrow
    nty = nn(nt_, yr)
    arrive(ps)
    ps = gather_stage(links, "x", yc.at[1], xregion(links))

    def image_free(lanes):
        yy[:, lanes] = nn(low, aec[:, lanes])
    chunks(image_free)
    arrive(ps)
    ps = gather_stage(links, "k", yc.at[1], kregion(links))
    ss = small_back(links, ss, sz, sres)
    arrive(ps)
    arrive(ss)
    head, nd = coupling(low, nt_, att, sres[:, 128:128 + B], sres[:, 0:B])
    left = jnp.concatenate([nty + nn(nd, kr), kr], axis=0).T

    def last(lanes):
        kcl = kc[:, lanes]
        hcl = nn(nt_, yy[:, lanes] - yc[1, :, lanes]) + nn(nd, kcl)
        o_ref[:, lanes] = o_ref[:, lanes] - nn(left, jnp.concatenate([kcl, hcl], axis=0))
    chunks(last)

    @pl.when(y == 0)
    def _():
        for j in range(1, NY):
            yscatter(j, lo, j).wait_send()
            yscatter(j, hi, NY + j).wait_send()

    @pl.when(row == 0)
    def _():
        for copy in core_copies:
            copy.wait_send()

    @pl.when(origin)
    def _():
        for j in range(1, NX):
            xscatter(j, lo, j).wait_send()
            xscatter(j, hi, NX + j).wait_send()

    @pl.when(z == 0)
    def _():
        for j in range(1, NZ):
            zscatter(j, lo, j).wait_send()
            zscatter(j, hi, NZ + j).wait_send()

    links.finish()


def local(matrix):
    vmem = pltpu.VMEM

    def ysum_buffers(lead, n):
        return [vmem(lead + (n, B, 256), F32), vmem(lead + (NY, n, 24, 128), F32), vmem(lead + (n, B, 256), F32)]

    return pl.pallas_call(
        body,
        out_shape=jax.ShapeDtypeStruct((ROWS, COLS), F32),
        in_specs=[pl.BlockSpec(memory_space=pltpu.VMEM)],
        out_specs=pl.BlockSpec(memory_space=pltpu.VMEM),
        scratch_shapes=[
            vmem((3, B, ROWS), F32), vmem((3, B, ROWS), F32), vmem((3, B, COLS), F32),
            vmem((3, 48, COLS), F32), vmem((3, 48, 512), F32),
            vmem((2, B, COLS), F32), vmem((2, 48, COLS), F32), vmem((2, 48, COLS), F32),
            vmem((2, NX, 48, 512), F32), vmem((2, 48, 512), F32), vmem((2, NZ, 24, 128), F32), vmem((2, B, COLS), F32),
            *ysum_buffers((2,), 1), *ysum_buffers((2,), 1), *ysum_buffers((1,), 2), *ysum_buffers((), 2),
            vmem((B, 256), F32), vmem((48, 256), F32), vmem((NX, 48, 256), F32), vmem((NZ, 48, 256), F32), vmem((B, 256), F32),
            vmem((2, B, COLS), F32), vmem((2, B, ROWS), F32), vmem((B, COLS), F32), vmem((B, ROWS), F32),
            vmem((B, COLS), F32), vmem((B, COLS), F32), vmem((B, COLS), F32), vmem((B, 128), F32),
            pltpu.SemaphoreType.DMA((SEND_SEMS,)), pltpu.SemaphoreType.DMA((SEND_SEMS,)),
        ],
        compiler_params=pltpu.CompilerParams(
            collective_id=0, has_side_effects=True, vmem_limit_bytes=56 * 1024 * 1024),
        name="two_panels",
    )(matrix)


def solution(mesh):
    return jax.shard_map(local, mesh=mesh, in_specs=(P("row", "col"),), out_specs=P("row", "col"), check_vma=False)
```

time: 188 us -> 153 us (0.81)
  Pallas kernels: 183 us -> 150 us
    pallas_call x1, Pallas kernels: 183 us -> 150 us  [local(): pl.pallas_call(body, out_shape=jax.ShapeDtypeStruct((ROWS, COLS), F32), i...]
where the time goes in v2:
time: 153 us
  Pallas kernels  150 us (98%)
  local copies, waits for them, and re-layouts  3.14 us (2%)
    pallas_call x1, Pallas kernels, local(): pl.pallas_call(body, out_shape=jax.ShapeDtypeStruct((ROWS, COLS), F32), i...  150 us
    unnamed x1, local copies, waits for them, and re-layouts  3.14 us

profile of v2, /device:TPU:1, one launch (start us, length us, event | category | flops | bytes accessed | tf_op | source)
XLA Modules:
  0.0 153.1 jit_solution(15893698622240410432)
XLA Ops:
  0.0 149.9 %two_panels.1 = f32[256,2048]{1,0:T(8,128)} custom-call(f32[256,2048]{1,0:T(8,128)} %a_ref.1), custom_call_target="tpu_custom_call" | custom-call | tf_op jit(solution)/shard_map/two_panels/pallas_call | solution.py:605
  149.9 3.1 %copy.3 = f32[256,2048]{1,0:T(8,128)} copy(f32[256,2048]{1,0:T(8,128)} %two_panels.1) | data formatting | bytes 4194304

commit v3 on v2

--- a/solution.py
+++ b/solution.py
@@ -13,7 +13,7 @@
 HIGH = lax.Precision.HIGHEST
 MESH = pl.DeviceIdType.MESH
 
-SEND_SEMS = 320
+SEND_SEMS = 400
 
 
 def nn(a, b):
@@ -162,26 +162,21 @@
     return gather_stage(links, "z", out, region)
 
 
-def small_core(links, src, bufk):
-    rows = pl.ds(pl.multiple_of(48 * (1 - links.k), 8), 48)
-    return exchange(links, "k", lambda j: src.at[rows, :], lambda j: bufk)
-
-
-def small_x(links, copies, src, bufk, parts):
+def small_core(links, src, parts):
+    parts[links.k] = src[ypiece(links.y)]
+    view = parts.at[links.k]
+    return exchange(links, "k", lambda j: view, lambda j: view)
+
+
+def small_next(links, copies, kind, before, parts):
     arrive(copies)
-    parts[links.x] = src[pl.ds(pl.multiple_of(48 * links.k, 8), 48), :] + bufk[...]
-    view = parts.at[links.x]
-    return exchange(links, "x", lambda j: view, lambda j: view)
-
-
-def small_z(links, copies, xparts, parts):
-    arrive(copies)
-    total = xparts[0]
-    for j in range(1, NX):
-        total = total + xparts[j]
-    parts[links.z] = total
-    view = parts.at[links.z]
-    return exchange(links, "z", lambda j: view, lambda j: view)
+    total = before[0]
+    for j in range(1, before.shape[0]):
+        total = total + before[j]
+    here = getattr(links, kind)
+    parts[here] = total
+    view = parts.at[here]
+    return exchange(links, kind, lambda j: view, lambda j: view)
 
 
 def small_back(links, copies, zparts, out):
@@ -189,8 +184,9 @@
     total = zparts[0]
     for j in range(1, NZ):
         total = total + zparts[j]
-    out[kregion(links)] = total
-    return gather_stage(links, "k", out, kregion(links))
+    mine = ypiece(links.y)
+    out[mine] = total
+    return gather_stage(links, "y", out, mine)
 
 
 def factor_block(b, carry):
@@ -251,13 +247,13 @@
     _, v, e, low = state
     low = pltpu.roll(low, 96, axis=1)[:, 0:B]
     v = pltpu.roll(v, 96, axis=1)
-    return low, nn(v.T[0:B], e)[:, 0:B]
+    return low, nn(v.T[0:B], e)[:, 0:B], e[:, 0:B]
 
 
 def body(a_ref, o_ref, wsrc, wr, wc, stgk, stgx,
          part, bufk, sumk, bufx, sumx, bufz, yc,
-         gsrc, gbuf, gres, rsrc, rbuf, rres, csrc, cbuf, cres, esrc, ebuf, eres,
-         ssrc, sbufk, sx, sz, sres,
+         gsrc, gbuf, gres, rsrc, rbuf, rres, csrc, cbuf, cres, esrc, ebuf, eres, fsrc, fbuf, fres,
+         ssrc, sk, sx, sz, sres,
          pcs, prs, aec, aer, yy, kc, hc, sq, send, recv):
     links = Links(send, recv)
     x, z, k, y, row = links.x, links.z, links.k, links.y, links.row
@@ -278,8 +274,8 @@
 
     ysc = links.sems(2 * NY)
     core = links.sems(3)
-    xsc = links.sems(2 * NX)
-    zsc = links.sems(2 * NZ)
+    xsc = links.sems(3 * NX)
+    zsc = links.sems(3 * NZ)
     mine = ypiece(y)
 
     def yscatter(j, part_, sem):
@@ -290,14 +286,14 @@
                    links.copy(a_ref.at[pl.ds(144, 48), :], stgk.at[1], core + 1, "k", 1),
                    links.copy(a_ref.at[pl.ds(240, 16), :], stgk.at[2, pl.ds(0, 16), :], core + 2, "k", 1)]
 
-    def xscatter(j, part_, sem):
-        return links.copy(stgk.at[part_, :, pl.ds(512 * j, 512)], stgx.at[part_], xsc + sem, "x", j)
-
-    def zscatter(j, part_, sem):
+    def xscatter(j, g):
+        return links.copy(stgk.at[g, :, pl.ds(512 * j, 512)], stgx.at[g], xsc + g * NX + j, "x", j)
+
+    def zscatter(j, g):
         rows, lanes = zpiece(j)
         to_rows = pl.ds(pl.multiple_of(48 * k + 24 * (j % 2), 8), 24)
         to_lanes = pl.ds(pl.multiple_of(512 * x + 128 * (j // 2), 128), 128)
-        return links.copy(stgx.at[part_, rows, lanes], wc.at[part_, to_rows, to_lanes], zsc + sem, "z", j)
+        return links.copy(stgx.at[g, rows, lanes], wc.at[g, to_rows, to_lanes], zsc + g * NZ + j, "z", j)
 
     def y_out(part_, g):
         @pl.when(y == 0)
@@ -315,29 +311,28 @@
 
         return gather_stage(links, "y", wr, piece)
 
-    def x_out(part_, g):
+    def x_out(g):
         @pl.when(origin)
         def _():
             @pl.when(k == 1)
             def _():
-                for copy in (core_copies[:1] if g == 0 else core_copies[1:]):
-                    copy.wait_recv()
+                core_copies[g].wait_recv()
             for j in range(1, NX):
-                xscatter(j, part_, g * NX + j).start()
-            stgx[part_] = stgk[part_, :, 0:512]
-
-    def z_out(part_, g):
+                xscatter(j, g).start()
+            stgx[g] = stgk[g, :, 0:512]
+
+    def z_out(g):
         @pl.when(z == 0)
         def _():
             @pl.when(x != 0)
             def _():
-                links.copy(stgx.at[part_], stgx.at[part_], xsc + g * NX + x, "x", 0).wait_recv()
+                links.copy(stgx.at[g], stgx.at[g], xsc + g * NX + x, "x", 0).wait_recv()
             for j in range(1, NZ):
-                zscatter(j, part_, g * NZ + j).start()
-            wc[(part_,) + zregion(links)] = stgx[(part_,) + zpiece(0)]
-
-    def z_in(part_, g):
-        region = (part_,) + zregion(links)
+                zscatter(j, g).start()
+            wc[(g,) + zregion(links)] = stgx[(g,) + zpiece(0)]
+
+    def z_in(g):
+        region = (g,) + zregion(links)
 
         @pl.when(z != 0)
         def _():
@@ -351,14 +346,13 @@
     def _():
         core_copies[0].start()
         stgk[0] = a_ref[0:48, :]
-
-    x_out(lo, 0)
-    wr_lo = y_in(lo, 0)
-
-    @pl.when(row == 0)
-    def _():
         for copy in core_copies[1:]:
             copy.start()
+
+    x_out(0)
+
+    @pl.when(row == 0)
+    def _():
         stgk[1] = a_ref[96:144, :]
         stgk[2] = a_ref[192:240, :]
 
@@ -366,14 +360,10 @@
     def _():
         stgk[2, 16:48, :] = a_ref[0:32, :]
 
-    @pl.when(y == 0)
-    def _():
-        t = a_ref[:, 0:384].T
-        wsrc[1] = t[B:2 * B]
-        wsrc[2] = t[2 * B:3 * B]
-
-    z_out(lo, 0)
-    y_out(hi, 1)
+    wr_lo = y_in(lo, 0)
+    x_out(1)
+    x_out(2)
+    z_out(0)
 
     gl_r = row * ROWS + lax.broadcasted_iota(jnp.int32, (B, ROWS), 1)
     gl_c = y * COLS + lax.broadcasted_iota(jnp.int32, (B, COLS), 1)
@@ -422,95 +412,105 @@
     prs[0] = jnp.where(gl_r >= B, wr[0], 0.0)
     product_cols(prs[0], a_ref, part.at[0])
     ps = psum_core(links, part.at[0], bufk.at[0])
-    wlo = z_in(lo, 0)
+
+    @pl.when(y == 0)
+    def _():
+        t = a_ref[:, 0:384].T
+        wsrc[1] = t[B:2 * B]
+        wsrc[2] = t[2 * B:3 * B]
+
+    y_out(hi, 1)
+    z_out(1)
+    z_out(2)
+    w0 = z_in(0)
     ps = psum_x(links, ps, part.at[0], bufk.at[0], sumk.at[0], bufx.at[0])
-    x_out(hi, 1)
+    arrive(w0)
+    w0 = gather_stage(links, "x", wc, (0,) + xregion(links))
+    ps = psum_z(links, ps, sumk.at[0], bufx.at[0], sumx.at[0], bufz.at[0])
     wr_hi = y_in(hi, 1)
-    arrive(wlo)
-    wlo = gather_stage(links, "x", wc, (lo,) + xregion(links))
-    ps = psum_z(links, ps, sumk.at[0], bufx.at[0], sumx.at[0], bufz.at[0])
-    arrive(wlo)
-    wlo = gather_stage(links, "k", wc, (lo,) + kregion(links))
-    z_out(hi, 1)
-    arrive(wlo)
+    arrive(w0)
+    w0 = gather_stage(links, "k", wc, (0,) + kregion(links))
+    arrive(w0)
     pcs[0] = jnp.where(gl_c >= B, wc[0], 0.0)
     gsrc[0, 0, :, 0:128] = widen(product_rows(pcs.at[0], pcs.at[0], B))
     gsrc[0, 0, :, 128:256] = col_square(pcs.at[0], B)
     gs = ysum_start(links, gsrc.at[0], gbuf.at[0])
-    whi = z_in(hi, 1)
     ps = psum_back_z(links, ps, sumx.at[0], bufz.at[0], yc.at[0])
     rsrc[0, 0] = product_rows(pcs.at[0], a_ref, ROWS)
     gs = ysum_mid(links, gs, gsrc.at[0], gbuf.at[0], gres.at[0])
     rs = ysum_start(links, rsrc.at[0], rbuf.at[0])
     arrive(ps)
     ps = gather_stage(links, "x", yc.at[0], xregion(links))
-    arrive(whi)
-    whi = gather_stage(links, "x", wc, (hi,) + xregion(links))
+    w1 = z_in(1)
     arrive(gs)
     top = gres[0, 0, :, 128:256]
-    state = factor_start(gres[0, 0, :, 0:128], top)
+    state = factor_some(0, 2, factor_start(gres[0, 0, :, 0:128], top))
     arrive(ps)
     ps = gather_stage(links, "k", yc.at[0], kregion(links))
-    state = factor_some(0, 4, state)
-    arrive(whi)
-    whi = gather_stage(links, "k", wc, (hi,) + kregion(links))
+    arrive(w1)
+    w1 = gather_stage(links, "x", wc, (1,) + xregion(links))
     arrive(ps)
-    arrive(whi)
     csrc[0, 0, :, 0:128] = widen(product_rows(pcs.at[0], yc.at[0], B))
     csrc[0, 0, :, 128:256] = col_square(yc.at[0], B)
-    csrc[0, 1, :, 0:128] = col_square(wc.at[1], B)
-    csrc[0, 1, :, 128:256] = col_square(yc.at[0], 2 * B)
     cs = ysum_start(links, csrc.at[0], cbuf.at[0])
     rs = ysum_mid(links, rs, rsrc.at[0], rbuf.at[0], rres.at[0])
-    state = factor_some(4, 8, state)
+    state = factor_some(2, 6, state)
+    w2 = z_in(2)
     cs = ysum_mid(links, cs, csrc.at[0], cbuf.at[0], cres.at[0])
-    esrc[0, :, 0:128] = col_square(wc.at[0], 2 * B)
-    esrc[0, :, 128:256] = col_square(wc.at[1], 2 * B)
-    esrc[1, :, 0:128] = col_square(wc.at[2], 2 * B)
-    esrc[1, :, 128:256] = jnp.zeros((B, 128), F32)
-    es = ysum_start(links, esrc, ebuf)
-    state = factor_some(8, 12, state)
-    low, nt_ = factor_end(state)
+    arrive(w1)
+    w1 = gather_stage(links, "k", wc, (1,) + kregion(links))
+    state = factor_some(6, 12, state)
+    low, nt_, inv = factor_end(state)
     unit = unit_part(low, B)
     kr = make_k(unit, 0)
-
-    def image(lanes):
-        yy[:, lanes] = nn(low, wc[1, :, lanes]) - yc[0, :, lanes]
-    chunks(image)
+    arrive(w1)
+    esrc[0, :, 0:128] = col_square(wc.at[1], B)
+    esrc[0, :, 128:256] = col_square(yc.at[0], 2 * B)
+    esrc[1, :, 0:128] = col_square(wc.at[0], 2 * B)
+    esrc[1, :, 128:256] = col_square(wc.at[1], 2 * B)
+    es = ysum_start(links, esrc, ebuf)
     arrive(rs)
-    arrive(wr_hi)
-    yr = nn(low, wr[1]) - rres[0, 0]
-    es = ysum_mid(links, es, esrc, ebuf, eres)
     arrive(cs)
 
-    def coupling(low, nt_, att, yt, phi):
-        head = nn(low, att) - yt
-        c = nt(head, low) - nt(low, yt) + phi
-        return head, -0.5 * nt(nn(nt_, c), nt_)
-
-    head, nd = coupling(low, nt_, cres[0, 1, :, 0:B], cres[0, 0, :, 128:128 + B], cres[0, 0, :, 0:B])
-    kt = low - top[:, 0:B]
-    ht = nn(nt_, head) + nn(nd, kt)
-    rows1 = jnp.concatenate([ht, kt], axis=0).T
+    yt, phi = cres[0, 0, :, 128:128 + B], cres[0, 0, :, 0:B]
+    of_k = -nn(inv, nt(nt(yt, low) - phi, nt_))
+    of_both = jnp.concatenate([inv, of_k], axis=1)
 
     def next_panel(lanes):
-        hcl = nn(nt_, yy[:, lanes]) + nn(nd, kc[:, lanes])
-        hc[:, lanes] = hcl
-        fresh = wc[1, :, lanes] - nn(rows1, jnp.concatenate([kc[:, lanes], hcl], axis=0))
-        pcs[1, :, lanes] = fresh
+        pcs[1, :, lanes] = nn(of_both, jnp.concatenate([yc[0, :, lanes], kc[:, lanes]], axis=0))
     chunks(next_panel)
     pcs[1] = jnp.where(gl_c >= 2 * B, pcs[1], 0.0)
     gsrc[1, 0, :, 0:128] = widen(product_rows(pcs.at[1], pcs.at[1], B))
     gsrc[1, 0, :, 128:256] = col_square(pcs.at[1], 2 * B)
     gs = ysum_start(links, gsrc.at[1], gbuf.at[1])
+    yrow = rres[0, 0]
+    prs[1] = jnp.where(gl_r >= 2 * B, nn(of_both, jnp.concatenate([yrow, kr], axis=0)), 0.0)
+    es = ysum_mid(links, es, esrc, ebuf, eres)
+    arrive(w2)
+    w2 = gather_stage(links, "x", wc, (2,) + xregion(links))
+
+    def image(lanes):
+        yy[:, lanes] = nn(low, wc[1, :, lanes]) - yc[0, :, lanes]
+    chunks(image)
+    arrive(wr_hi)
+    yr = nn(low, wr[1]) - yrow
+
+    def coupling(low, nt_, att, yt, phi):
+        c = nt(nn(low, att) - yt, low) - nt(low, yt) + phi
+        return -0.5 * nt(nn(nt_, c), nt_)
+
+    arrive(es)
+    nd = coupling(low, nt_, eres[0, :, 0:B], yt, phi)
     hr = nn(nt_, yr) + nn(nd, kr)
     right_r = jnp.concatenate([kr, hr], axis=0)
-    prs[1] = jnp.where(gl_r >= 2 * B, wr[1] - nn(rows1, right_r), 0.0)
     left = jnp.concatenate([hr, kr], axis=0).T
+    of_h = jnp.concatenate([nt_, nd], axis=1)
 
     def update(lanes):
-        right = jnp.concatenate([kc[:, lanes], hc[:, lanes]], axis=0)
-        o_ref[:, lanes] = a_ref[:, lanes] - nn(left, right)
+        kcl = kc[:, lanes]
+        hcl = nn(of_h, jnp.concatenate([yy[:, lanes], kcl], axis=0))
+        hc[:, lanes] = hcl
+        o_ref[:, lanes] = a_ref[:, lanes] - nn(left, jnp.concatenate([kcl, hcl], axis=0))
     chunks(update)
 
     rsrc[1, 0] = product_rows(pcs.at[1], o_ref, ROWS)
@@ -518,55 +518,64 @@
     product_cols(prs[1], o_ref, part.at[1])
     ps = psum_core(links, part.at[1], bufk.at[1])
     gs = ysum_mid(links, gs, gsrc.at[1], gbuf.at[1], gres.at[1])
+    arrive(w2)
+    w2 = gather_stage(links, "k", wc, (2,) + kregion(links))
     ps = psum_x(links, ps, part.at[1], bufk.at[1], sumk.at[1], bufx.at[1])
-    arrive(es)
-    kt = -eres[0, :, 0:B]
-    ht = nn(nt_, nn(low, eres[0, :, 128:128 + B]) - cres[0, 1, :, 128:128 + B]) + nn(nd, kt)
+    kt = -eres[1, :, 0:B]
+    ht = nn(nt_, nn(low, eres[1, :, 128:128 + B]) - eres[0, :, 128:128 + B]) + nn(nd, kt)
     rows2 = jnp.concatenate([ht, kt], axis=0).T
-    att = eres[1, :, 0:B] - nn(rows2, jnp.concatenate([kt, ht], axis=0))
     aer[...] = wr[2] - nn(rows2, right_r)
-    rs = ysum_mid(links, rs, rsrc.at[1], rbuf.at[1], rres.at[1])
+    arrive(w2)
+    fsrc[0, :, 0:128] = col_square(wc.at[2], 2 * B)
+    fsrc[0, :, 128:256] = jnp.zeros((B, 128), F32)
+    fs = ysum_start(links, fsrc, fbuf)
 
     def next_rows(lanes):
         aec[:, lanes] = wc[2, :, lanes] - nn(rows2, jnp.concatenate([kc[:, lanes], hc[:, lanes]], axis=0))
     chunks(next_rows)
+    rs = ysum_mid(links, rs, rsrc.at[1], rbuf.at[1], rres.at[1])
     ps = psum_z(links, ps, sumk.at[1], bufx.at[1], sumx.at[1], bufz.at[1])
     arrive(gs)
     top = gres[1, 0, :, 128:256]
-    state = factor_some(0, 6, factor_start(gres[1, 0, :, 0:128], top))
+    state = factor_some(0, 5, factor_start(gres[1, 0, :, 0:128], top))
     arrive(rs)
     yrow = rres[1, 0]
     none = jnp.zeros((B, ROWS), F32)
     ssrc[:, 0:128] = widen(nt(prs[1], yrow))
     ssrc[:, 128:256] = (jnp.where(row == 0, square(jnp.concatenate([yrow, none], axis=1), 2 * B), 0.0)
                         + jnp.where(row == 1, square(jnp.concatenate([none, yrow], axis=1), 2 * B), 0.0))
-    ss = small_core(links, ssrc, sbufk)
-    state = factor_some(6, 8, state)
-    ss = small_x(links, ss, ssrc, sbufk, sx)
+    ss = small_core(links, ssrc, sk)
+    fs = ysum_mid(links, fs, fsrc, fbuf, fres)
     ps = psum_back_z(links, ps, sumx.at[1], bufz.at[1], yc.at[1])
-    state = factor_some(8, 12, state)
-    ss = small_z(links, ss, sx, sz)
-    low, nt_ = factor_end(state)
+    ss = small_next(links, ss, "x", sk, sx)
+    state = factor_some(5, 9, state)
+    ss = small_next(links, ss, "z", sx, sz)
+    arrive(ps)
+    ps = gather_stage(links, "x", yc.at[1], xregion(links))
+    state = factor_some(9, 12, state)
+    kt1, ht1 = kt, ht
+    low, nt_, _ = factor_end(state)
+    ss = small_back(links, ss, sz, sres)
+    arrive(ps)
+    ps = gather_stage(links, "k", yc.at[1], kregion(links))
     kr = make_k(unit_part(low, 2 * B), 1)
     yr = nn(low, aer[...]) - yrow
     nty = nn(nt_, yr)
-    arrive(ps)
-    ps = gather_stage(links, "x", yc.at[1], xregion(links))
 
     def image_free(lanes):
         yy[:, lanes] = nn(low, aec[:, lanes])
     chunks(image_free)
-    arrive(ps)
-    ps = gather_stage(links, "k", yc.at[1], kregion(links))
-    ss = small_back(links, ss, sz, sres)
+    arrive(fs)
+    att = fres[0, :, 0:B] - nn(rows2, jnp.concatenate([kt1, ht1], axis=0))
     arrive(ps)
     arrive(ss)
-    head, nd = coupling(low, nt_, att, sres[:, 128:128 + B], sres[:, 0:B])
+    nd = coupling(low, nt_, att, sres[:, 128:128 + B], sres[:, 0:B])
     left = jnp.concatenate([nty + nn(nd, kr), kr], axis=0).T
+    of_h = jnp.concatenate([nt_, nd], axis=1)
 
     def last(lanes):
         kcl = kc[:, lanes]
-        hcl = nn(nt_, yy[:, lanes] - yc[1, :, lanes]) + nn(nd, kcl)
+        hcl = nn(of_h, jnp.concatenate([yy[:, lanes] - yc[1, :, lanes], kcl], axis=0))
         o_ref[:, lanes] = o_ref[:, lanes] - nn(left, jnp.concatenate([kcl, hcl], axis=0))
     chunks(last)
 
@@ -584,14 +593,14 @@
     @pl.when(origin)
     def _():
         for j in range(1, NX):
-            xscatter(j, lo, j).wait_send()
-            xscatter(j, hi, NX + j).wait_send()
+            for g in range(3):
+                xscatter(j, g).wait_send()
 
     @pl.when(z == 0)
     def _():
         for j in range(1, NZ):
-            zscatter(j, lo, j).wait_send()
-            zscatter(j, hi, NZ + j).wait_send()
+            for g in range(3):
+                zscatter(j, g).wait_send()
 
     links.finish()
 
@@ -612,8 +621,8 @@
             vmem((3, 48, COLS), F32), vmem((3, 48, 512), F32),
             vmem((2, B, COLS), F32), vmem((2, 48, COLS), F32), vmem((2, 48, COLS), F32),
             vmem((2, NX, 48, 512), F32), vmem((2, 48, 512), F32), vmem((2, NZ, 24, 128), F32), vmem((2, B, COLS), F32),
-            *ysum_buffers((2,), 1), *ysum_buffers((2,), 1), *ysum_buffers((1,), 2), *ysum_buffers((), 2),
-            vmem((B, 256), F32), vmem((48, 256), F32), vmem((NX, 48, 256), F32), vmem((NZ, 48, 256), F32), vmem((B, 256), F32),
+            *ysum_buffers((2,), 1), *ysum_buffers((2,), 1), *ysum_buffers((1,), 1), *ysum_buffers((), 2), *ysum_buffers((), 1),
+            vmem((B, 256), F32), vmem((2, 24, 128), F32), vmem((NX, 24, 128), F32), vmem((NZ, 24, 128), F32), vmem((B, 256), F32),
             vmem((2, B, COLS), F32), vmem((2, B, ROWS), F32), vmem((B, COLS), F32), vmem((B, ROWS), F32),
             vmem((B, COLS), F32), vmem((B, COLS), F32), vmem((B, COLS), F32), vmem((B, 128), F32),
             pltpu.SemaphoreType.DMA((SEND_SEMS,)), pltpu.SemaphoreType.DMA((SEND_SEMS,)),

time: 153 us -> 138 us (0.902)
  Pallas kernels: 150 us -> 134 us
    pallas_call x1, Pallas kernels: 150 us -> 134 us  [local(): pl.pallas_call(body, out_shape=jax.ShapeDtypeStruct((ROWS, COLS), F32), i...]
where the time goes in v3:
time: 138 us; the launch traced here: 137 us
  Pallas kernels  134 us (97%)
  local copies, waits for them, and re-layouts  3.14 us (2%)
    pallas_call x1, Pallas kernels, local(): pl.pallas_call(body, out_shape=jax.ShapeDtypeStruct((ROWS, COLS), F32), i...  134 us
    unnamed x1, local copies, waits for them, and re-layouts  3.14 us

profile of v3, /device:TPU:1, one launch (start us, length us, event | category | flops | bytes accessed | tf_op | source)
XLA Modules:
  0.0 137.3 jit_solution(7671610187377336304)
XLA Ops:
  0.0 134.2 %two_panels.1 = f32[256,2048]{1,0:T(8,128)} custom-call(f32[256,2048]{1,0:T(8,128)} %a_ref.1), custom_call_target="tpu_custom_call" | custom-call | tf_op jit(solution)/shard_map/two_panels/pallas_call | solution.py:614
  134.2 3.1 %copy.3 = f32[256,2048]{1,0:T(8,128)} copy(f32[256,2048]{1,0:T(8,128)} %two_panels.1) | data formatting | bytes 4194304

commit v4 on v3

--- a/solution.py
+++ b/solution.py
@@ -13,7 +13,8 @@
 HIGH = lax.Precision.HIGHEST
 MESH = pl.DeviceIdType.MESH
 
-SEND_SEMS = 400
+SEMS = 52
+METER = 768
 
 
 def nn(a, b):
@@ -25,8 +26,8 @@
 
 
 class Links:
-    def __init__(self, send, recv):
-        self.send, self.recv, self.count, self.open = send, recv, 0, []
+    def __init__(self, send, recv, meter):
+        self.send, self.recv, self.meter, self.count, self.open = send, recv, meter, 0, []
         row, self.y = lax.axis_index("row"), lax.axis_index("col")
         self.row = row
         self.x, self.z, self.k = row // 16, (row // 2) % 8, row % 2
@@ -53,29 +54,39 @@
             src_ref=src, dst_ref=dst, send_sem=self.send.at[sem], recv_sem=self.recv.at[sem],
             device_id=self.at(kind, j), device_id_type=MESH)
 
+    def take(self, sem, words):
+        whole = self.meter.at[pl.ds(0, words // 128), :]
+        pltpu.make_async_copy(whole, whole, sem).wait()
+
     def finish(self):
-        for copy in self.open:
-            copy.wait_send()
+        for sem, words in self.open:
+            self.take(self.send.at[sem], words)
 
 
 SIZE = {"x": NX, "z": NZ, "y": NY, "k": 2}
 
 
+def words_of(ref):
+    n = 1
+    for size in ref.shape:
+        n *= size
+    return n
+
+
 def exchange(links, kind, src_of, dst_of):
-    n = SIZE[kind]
-    first = links.sems(n)
-    copies = []
-    for j in range(1, n):
-        copy = links.copy(src_of(j), dst_of(j), first + j, kind, j)
-        copy.start()
-        copies.append(copy)
-    links.open += copies
-    return copies
-
-
-def arrive(copies):
-    for copy in copies:
-        copy.wait_recv()
+    sem = links.sems(1)
+    words = 0
+    for j in range(1, SIZE[kind]):
+        src = src_of(j)
+        words += words_of(src)
+        links.copy(src, dst_of(j), sem, kind, j).start()
+    links.open.append((sem, words))
+    return links, sem, words
+
+
+def arrive(coming):
+    links, sem, words = coming
+    links.take(links.recv.at[sem], words)
 
 
 def place(links, kind, j):
@@ -254,8 +265,8 @@
          part, bufk, sumk, bufx, sumx, bufz, yc,
          gsrc, gbuf, gres, rsrc, rbuf, rres, csrc, cbuf, cres, esrc, ebuf, eres, fsrc, fbuf, fres,
          ssrc, sk, sx, sz, sres,
-         pcs, prs, aec, aer, yy, kc, hc, sq, send, recv):
-    links = Links(send, recv)
+         pcs, prs, aec, aer, yy, kc, hc, sq, meter, send, recv):
+    links = Links(send, recv, meter)
     x, z, k, y, row = links.x, links.z, links.k, links.y, links.row
 
     barrier = pltpu.get_barrier_semaphore()
@@ -272,42 +283,42 @@
     lo, hi = (pl.ds(0, 1), pl.ds(1, 2))
     origin = (x == 0) & (z == 0)
 
-    ysc = links.sems(2 * NY)
+    ysc = links.sems(2)
     core = links.sems(3)
-    xsc = links.sems(3 * NX)
-    zsc = links.sems(3 * NZ)
+    xsc = links.sems(3)
+    zsc = links.sems(3)
     mine = ypiece(y)
 
-    def yscatter(j, part_, sem):
+    def yscatter(j, part_, g):
         piece = (part_,) + ypiece(j)
-        return links.copy(wsrc.at[piece], wr.at[piece], ysc + sem, "y", j)
+        return links.copy(wsrc.at[piece], wr.at[piece], ysc + g, "y", j)
 
     core_copies = [links.copy(a_ref.at[pl.ds(48, 48), :], stgk.at[0], core, "k", 1),
                    links.copy(a_ref.at[pl.ds(144, 48), :], stgk.at[1], core + 1, "k", 1),
                    links.copy(a_ref.at[pl.ds(240, 16), :], stgk.at[2, pl.ds(0, 16), :], core + 2, "k", 1)]
 
     def xscatter(j, g):
-        return links.copy(stgk.at[g, :, pl.ds(512 * j, 512)], stgx.at[g], xsc + g * NX + j, "x", j)
+        return links.copy(stgk.at[g, :, pl.ds(512 * j, 512)], stgx.at[g], xsc + g, "x", j)
 
     def zscatter(j, g):
         rows, lanes = zpiece(j)
         to_rows = pl.ds(pl.multiple_of(48 * k + 24 * (j % 2), 8), 24)
         to_lanes = pl.ds(pl.multiple_of(512 * x + 128 * (j // 2), 128), 128)
-        return links.copy(stgx.at[g, rows, lanes], wc.at[g, to_rows, to_lanes], zsc + g * NZ + j, "z", j)
+        return links.copy(stgx.at[g, rows, lanes], wc.at[g, to_rows, to_lanes], zsc + g, "z", j)
 
     def y_out(part_, g):
         @pl.when(y == 0)
         def _():
             wr[(part_,) + ypiece(0)] = wsrc[(part_,) + ypiece(0)]
             for j in range(1, NY):
-                yscatter(j, part_, g * NY + j).start()
+                yscatter(j, part_, g).start()
 
     def y_in(part_, g):
         piece = (part_,) + mine
 
         @pl.when(y != 0)
         def _():
-            links.copy(wr.at[piece], wr.at[piece], ysc + g * NY + y, "y", 0).wait_recv()
+            links.copy(wr.at[piece], wr.at[piece], ysc + g, "y", 0).wait_recv()
 
         return gather_stage(links, "y", wr, piece)
 
@@ -326,7 +337,7 @@
         def _():
             @pl.when(x != 0)
             def _():
-                links.copy(stgx.at[g], stgx.at[g], xsc + g * NX + x, "x", 0).wait_recv()
+                links.copy(stgx.at[g], stgx.at[g], xsc + g, "x", 0).wait_recv()
             for j in range(1, NZ):
                 zscatter(j, g).start()
             wc[(g,) + zregion(links)] = stgx[(g,) + zpiece(0)]
@@ -336,7 +347,7 @@
 
         @pl.when(z != 0)
         def _():
-            links.copy(wc.at[region], wc.at[region], zsc + g * NZ + z, "z", 0).wait_recv()
+            links.copy(wc.at[region], wc.at[region], zsc + g, "z", 0).wait_recv()
 
         return gather_stage(links, "z", wc, region)
 
@@ -361,8 +372,6 @@
         stgk[2, 16:48, :] = a_ref[0:32, :]
 
     wr_lo = y_in(lo, 0)
-    x_out(1)
-    x_out(2)
     z_out(0)
 
     gl_r = row * ROWS + lax.broadcasted_iota(jnp.int32, (B, ROWS), 1)
@@ -420,31 +429,29 @@
         wsrc[2] = t[2 * B:3 * B]
 
     y_out(hi, 1)
-    z_out(1)
-    z_out(2)
     w0 = z_in(0)
     ps = psum_x(links, ps, part.at[0], bufk.at[0], sumk.at[0], bufx.at[0])
     arrive(w0)
     w0 = gather_stage(links, "x", wc, (0,) + xregion(links))
     ps = psum_z(links, ps, sumk.at[0], bufx.at[0], sumx.at[0], bufz.at[0])
+    x_out(1)
     wr_hi = y_in(hi, 1)
     arrive(w0)
     w0 = gather_stage(links, "k", wc, (0,) + kregion(links))
+    ps = psum_back_z(links, ps, sumx.at[0], bufz.at[0], yc.at[0])
+    z_out(1)
     arrive(w0)
     pcs[0] = jnp.where(gl_c >= B, wc[0], 0.0)
     gsrc[0, 0, :, 0:128] = widen(product_rows(pcs.at[0], pcs.at[0], B))
     gsrc[0, 0, :, 128:256] = col_square(pcs.at[0], B)
     gs = ysum_start(links, gsrc.at[0], gbuf.at[0])
-    ps = psum_back_z(links, ps, sumx.at[0], bufz.at[0], yc.at[0])
     rsrc[0, 0] = product_rows(pcs.at[0], a_ref, ROWS)
-    gs = ysum_mid(links, gs, gsrc.at[0], gbuf.at[0], gres.at[0])
-    rs = ysum_start(links, rsrc.at[0], rbuf.at[0])
     arrive(ps)
     ps = gather_stage(links, "x", yc.at[0], xregion(links))
     w1 = z_in(1)
-    arrive(gs)
-    top = gres[0, 0, :, 128:256]
-    state = factor_some(0, 2, factor_start(gres[0, 0, :, 0:128], top))
+    gs = ysum_mid(links, gs, gsrc.at[0], gbuf.at[0], gres.at[0])
+    rs = ysum_start(links, rsrc.at[0], rbuf.at[0])
+    x_out(2)
     arrive(ps)
     ps = gather_stage(links, "k", yc.at[0], kregion(links))
     arrive(w1)
@@ -454,22 +461,34 @@
     csrc[0, 0, :, 128:256] = col_square(yc.at[0], B)
     cs = ysum_start(links, csrc.at[0], cbuf.at[0])
     rs = ysum_mid(links, rs, rsrc.at[0], rbuf.at[0], rres.at[0])
-    state = factor_some(2, 6, state)
-    w2 = z_in(2)
-    cs = ysum_mid(links, cs, csrc.at[0], cbuf.at[0], cres.at[0])
+    z_out(2)
+    arrive(gs)
+    top = gres[0, 0, :, 128:256]
+    state = factor_some(0, 6, factor_start(gres[0, 0, :, 0:128], top))
     arrive(w1)
     w1 = gather_stage(links, "k", wc, (1,) + kregion(links))
-    state = factor_some(6, 12, state)
-    low, nt_, inv = factor_end(state)
-    unit = unit_part(low, B)
-    kr = make_k(unit, 0)
+    state = factor_some(6, 8, state)
     arrive(w1)
     esrc[0, :, 0:128] = col_square(wc.at[1], B)
     esrc[0, :, 128:256] = col_square(yc.at[0], 2 * B)
     esrc[1, :, 0:128] = col_square(wc.at[0], 2 * B)
     esrc[1, :, 128:256] = col_square(wc.at[1], 2 * B)
     es = ysum_start(links, esrc, ebuf)
+    cs = ysum_mid(links, cs, csrc.at[0], cbuf.at[0], cres.at[0])
+    state = factor_some(8, 12, state)
+    low, nt_, inv = factor_end(state)
+    unit = unit_part(low, B)
+    kr = make_k(unit, 0)
+
+    def image(lanes):
+        yy[:, lanes] = nn(low, wc[1, :, lanes]) - yc[0, :, lanes]
+    chunks(image)
+    es = ysum_mid(links, es, esrc, ebuf, eres)
+    w2 = z_in(2)
     arrive(rs)
+    arrive(wr_hi)
+    yrow = rres[0, 0]
+    yr = nn(low, wr[1]) - yrow
     arrive(cs)
 
     yt, phi = cres[0, 0, :, 128:128 + B], cres[0, 0, :, 0:B]
@@ -483,17 +502,9 @@
     gsrc[1, 0, :, 0:128] = widen(product_rows(pcs.at[1], pcs.at[1], B))
     gsrc[1, 0, :, 128:256] = col_square(pcs.at[1], 2 * B)
     gs = ysum_start(links, gsrc.at[1], gbuf.at[1])
-    yrow = rres[0, 0]
     prs[1] = jnp.where(gl_r >= 2 * B, nn(of_both, jnp.concatenate([yrow, kr], axis=0)), 0.0)
-    es = ysum_mid(links, es, esrc, ebuf, eres)
     arrive(w2)
     w2 = gather_stage(links, "x", wc, (2,) + xregion(links))
-
-    def image(lanes):
-        yy[:, lanes] = nn(low, wc[1, :, lanes]) - yc[0, :, lanes]
-    chunks(image)
-    arrive(wr_hi)
-    yr = nn(low, wr[1]) - yrow
 
     def coupling(low, nt_, att, yt, phi):
         c = nt(nn(low, att) - yt, low) - nt(low, yt) + phi
@@ -506,16 +517,19 @@
     left = jnp.concatenate([hr, kr], axis=0).T
     of_h = jnp.concatenate([nt_, nd], axis=1)
 
-    def update(lanes):
+    prow = prs[1]
+
+    def update(i, acc):
+        lanes = pl.ds(pl.multiple_of(512 * i, 512), 512)
         kcl = kc[:, lanes]
         hcl = nn(of_h, jnp.concatenate([yy[:, lanes], kcl], axis=0))
         hc[:, lanes] = hcl
-        o_ref[:, lanes] = a_ref[:, lanes] - nn(left, jnp.concatenate([kcl, hcl], axis=0))
-    chunks(update)
-
-    rsrc[1, 0] = product_rows(pcs.at[1], o_ref, ROWS)
+        fresh = a_ref[:, lanes] - nn(left, jnp.concatenate([kcl, hcl], axis=0))
+        o_ref[:, lanes] = fresh
+        part[1, :, lanes] = nn(prow, fresh)
+        return acc + nt(pcs[1, :, lanes], fresh)
+    rsrc[1, 0] = lax.fori_loop(0, 4, update, jnp.zeros((B, ROWS), F32))
     rs = ysum_start(links, rsrc.at[1], rbuf.at[1])
-    product_cols(prs[1], o_ref, part.at[1])
     ps = psum_core(links, part.at[1], bufk.at[1])
     gs = ysum_mid(links, gs, gsrc.at[1], gbuf.at[1], gres.at[1])
     arrive(w2)
@@ -581,9 +595,8 @@
 
     @pl.when(y == 0)
     def _():
-        for j in range(1, NY):
-            yscatter(j, lo, j).wait_send()
-            yscatter(j, hi, NY + j).wait_send()
+        for g, panels in ((0, 1), (1, 2)):
+            links.take(send.at[ysc + g], (NY - 1) * panels * 24 * 128)
 
     @pl.when(row == 0)
     def _():
@@ -592,15 +605,13 @@
 
     @pl.when(origin)
     def _():
-        for j in range(1, NX):
-            for g in range(3):
-                xscatter(j, g).wait_send()
+        for g in range(3):
+            links.take(send.at[xsc + g], (NX - 1) * 48 * 512)
 
     @pl.when(z == 0)
     def _():
-        for j in range(1, NZ):
-            for g in range(3):
-                zscatter(j, g).wait_send()
+        for g in range(3):
+            links.take(send.at[zsc + g], (NZ - 1) * 24 * 128)
 
     links.finish()
 
@@ -625,7 +636,8 @@
             vmem((B, 256), F32), vmem((2, 24, 128), F32), vmem((NX, 24, 128), F32), vmem((NZ, 24, 128), F32), vmem((B, 256), F32),
             vmem((2, B, COLS), F32), vmem((2, B, ROWS), F32), vmem((B, COLS), F32), vmem((B, ROWS), F32),
             vmem((B, COLS), F32), vmem((B, COLS), F32), vmem((B, COLS), F32), vmem((B, 128), F32),
-            pltpu.SemaphoreType.DMA((SEND_SEMS,)), pltpu.SemaphoreType.DMA((SEND_SEMS,)),
+            vmem((METER, 128), F32),
+            pltpu.SemaphoreType.DMA((SEMS,)), pltpu.SemaphoreType.DMA((SEMS,)),
         ],
         compiler_params=pltpu.CompilerParams(
             collective_id=0, has_side_effects=True, vmem_limit_bytes=56 * 1024 * 1024),

time: 138 us -> 125 us (0.906)
  Pallas kernels: 134 us -> 122 us
    pallas_call x1, Pallas kernels: 134 us -> 122 us  [local(): pl.pallas_call(body, out_shape=jax.ShapeDtypeStruct((ROWS, COLS), F32), i...]
where the time goes in v4:
time: 125 us
  Pallas kernels  122 us (98%)
  local copies, waits for them, and re-layouts  3.14 us (3%)
    pallas_call x1, Pallas kernels, local(): pl.pallas_call(body, out_shape=jax.ShapeDtypeStruct((ROWS, COLS), F32), i...  122 us
    unnamed x1, local copies, waits for them, and re-layouts  3.14 us

profile of v4, /device:TPU:1, one launch (start us, length us, event | category | flops | bytes accessed | tf_op | source)
XLA Modules:
  0.0 125.2 jit_solution(11115002307002094271)
XLA Ops:
  0.0 122.0 %two_panels.1 = f32[256,2048]{1,0:T(8,128)} custom-call(f32[256,2048]{1,0:T(8,128)} %a_ref.1), custom_call_target="tpu_custom_call" | custom-call | tf_op jit(solution)/shard_map/two_panels/pallas_call | solution.py:625
  122.0 3.1 %copy.3 = f32[256,2048]{1,0:T(8,128)} copy(f32[256,2048]{1,0:T(8,128)} %two_panels.1) | data formatting | bytes 4194304

commit v5 on v4

--- a/solution.py
+++ b/solution.py
@@ -13,8 +13,8 @@
 HIGH = lax.Precision.HIGHEST
 MESH = pl.DeviceIdType.MESH
 
-SEMS = 52
-METER = 768
+SEMS = 53
+METER = 1344
 
 
 def nn(a, b):
@@ -138,6 +138,37 @@
         total = total + buf[j]
     res[mine] = total
     return gather_stage(links, "y", res, mine)
+
+
+def half_start(links, src, parts, head, sem):
+    rows = pl.ds(pl.multiple_of(48 * links.k, 8), 48)
+    parts[links.y] = src[rows, 0:128]
+    view = parts.at[links.y]
+    coming = exchange(links, "y", lambda j: view, lambda j: view)
+
+    @pl.when(links.y == 0)
+    def _():
+        head[...] = src[rows, 128:256]
+        for j in range(1, NY):
+            links.copy(head, head, sem, "y", j).start()
+
+    return coming
+
+
+def half_mid(links, coming, parts, head, sem, res):
+    rows = pl.ds(pl.multiple_of(48 * links.k, 8), 48)
+    arrive(coming)
+
+    @pl.when(links.y != 0)
+    def _():
+        links.copy(head, head, sem, "y", 0).wait_recv()
+
+    total = parts[0]
+    for j in range(1, NY):
+        total = total + parts[j]
+    res[rows, 0:128] = total
+    res[rows, 128:256] = head[...]
+    return gather_stage(links, "k", res, kregion(links))
 
 
 def psum_core(links, part, bufk):
@@ -263,9 +294,9 @@
 
 def body(a_ref, o_ref, wsrc, wr, wc, stgk, stgx,
          part, bufk, sumk, bufx, sumx, bufz, yc,
-         gsrc, gbuf, gres, rsrc, rbuf, rres, csrc, cbuf, cres, esrc, ebuf, eres, fsrc, fbuf, fres,
+         gsrc, gbuf, gres, rsrc, rbuf, rres, csrc, cparts, chead, cres, gparts, ghead, esrc, ebuf, eres, fsrc, fbuf, fres,
          ssrc, sk, sx, sz, sres,
-         pcs, prs, aec, aer, yy, kc, hc, sq, meter, send, recv):
+         pcs, prs, aec, aer, im, yy, kc, hc, sq, meter, send, recv):
     links = Links(send, recv, meter)
     x, z, k, y, row = links.x, links.z, links.k, links.y, links.row
 
@@ -284,6 +315,7 @@
     origin = (x == 0) & (z == 0)
 
     ysc = links.sems(2)
+    hsem = links.sems(2)
     core = links.sems(3)
     xsc = links.sems(3)
     zsc = links.sems(3)
@@ -351,7 +383,14 @@
 
         return gather_stage(links, "z", wc, region)
 
-    y_out(lo, 0)
+    def direct(j):
+        return links.copy(wsrc.at[lo], wr.at[lo], ysc, "y", j)
+
+    @pl.when(y == 0)
+    def _():
+        for j in (4, 3, 5, 2, 6, 1, 7):
+            direct(j).start()
+        wr[0] = wsrc[0]
 
     @pl.when(row == 0)
     def _():
@@ -371,7 +410,6 @@
     def _():
         stgk[2, 16:48, :] = a_ref[0:32, :]
 
-    wr_lo = y_in(lo, 0)
     z_out(0)
 
     gl_r = row * ROWS + lax.broadcasted_iota(jnp.int32, (B, ROWS), 1)
@@ -408,6 +446,11 @@
     def col_square(ref, at):
         return jnp.where(first_col, square(ref[:, 0:384], at), 0.0)
 
+    def scale_of(gram):
+        eye = lax.broadcasted_iota(jnp.int32, (B, 128), 0) == lane128
+        diagonal = jnp.sum(jnp.where(eye, gram, 0.0), axis=1, keepdims=True)
+        return lax.rsqrt(jnp.max(diagonal, axis=0, keepdims=True))
+
     def unit_part(chol, trail):
         wide = jnp.concatenate([widen(chol), jnp.zeros((B, 384), F32)], axis=1)
         return pltpu.roll(wide, trail, axis=1)
@@ -417,7 +460,10 @@
         kc[:, 0:512] = kc[:, 0:512] + jnp.where(first_col, unit, 0.0)
         return (jnp.where(row == 0, unit[:, 0:256], 0.0) + jnp.where(row == 1, unit[:, 256:512], 0.0)) - prs[p]
 
-    arrive(wr_lo)
+    @pl.when(y != 0)
+    def _():
+        links.copy(wr.at[lo], wr.at[lo], ysc, "y", 0).wait_recv()
+
     prs[0] = jnp.where(gl_r >= B, wr[0], 0.0)
     product_cols(prs[0], a_ref, part.at[0])
     ps = psum_core(links, part.at[0], bufk.at[0])
@@ -444,12 +490,12 @@
     pcs[0] = jnp.where(gl_c >= B, wc[0], 0.0)
     gsrc[0, 0, :, 0:128] = widen(product_rows(pcs.at[0], pcs.at[0], B))
     gsrc[0, 0, :, 128:256] = col_square(pcs.at[0], B)
-    gs = ysum_start(links, gsrc.at[0], gbuf.at[0])
+    gs = half_start(links, gsrc.at[0, 0], gparts, ghead, hsem + 1)
     rsrc[0, 0] = product_rows(pcs.at[0], a_ref, ROWS)
     arrive(ps)
     ps = gather_stage(links, "x", yc.at[0], xregion(links))
     w1 = z_in(1)
-    gs = ysum_mid(links, gs, gsrc.at[0], gbuf.at[0], gres.at[0])
+    gs = half_mid(links, gs, gparts, ghead, hsem + 1, gres.at[0, 0])
     rs = ysum_start(links, rsrc.at[0], rbuf.at[0])
     x_out(2)
     arrive(ps)
@@ -457,46 +503,50 @@
     arrive(w1)
     w1 = gather_stage(links, "x", wc, (1,) + xregion(links))
     arrive(ps)
-    csrc[0, 0, :, 0:128] = widen(product_rows(pcs.at[0], yc.at[0], B))
-    csrc[0, 0, :, 128:256] = col_square(yc.at[0], B)
-    cs = ysum_start(links, csrc.at[0], cbuf.at[0])
+    arrive(gs)
+    scale = scale_of(gres[0, 0, :, 0:128])
+    pcs[0] = pcs[0] * scale
+    prs[0] = prs[0] * scale
+    im[...] = yc[0] * scale
+    csrc[:, 0:128] = widen(product_rows(pcs.at[0], im, B))
+    csrc[:, 128:256] = col_square(im, B)
+    cs = half_start(links, csrc, cparts, chead, hsem)
     rs = ysum_mid(links, rs, rsrc.at[0], rbuf.at[0], rres.at[0])
     z_out(2)
-    arrive(gs)
-    top = gres[0, 0, :, 128:256]
-    state = factor_some(0, 6, factor_start(gres[0, 0, :, 0:128], top))
+    top = gres[0, 0, :, 128:256] * scale
+    state = factor_some(0, 6, factor_start(gres[0, 0, :, 0:128] * scale * scale, top))
     arrive(w1)
     w1 = gather_stage(links, "k", wc, (1,) + kregion(links))
     state = factor_some(6, 8, state)
     arrive(w1)
     esrc[0, :, 0:128] = col_square(wc.at[1], B)
-    esrc[0, :, 128:256] = col_square(yc.at[0], 2 * B)
-    esrc[1, :, 0:128] = col_square(wc.at[0], 2 * B)
+    esrc[0, :, 128:256] = col_square(im, 2 * B)
+    esrc[1, :, 0:128] = col_square(pcs.at[0], 2 * B)
     esrc[1, :, 128:256] = col_square(wc.at[1], 2 * B)
     es = ysum_start(links, esrc, ebuf)
-    cs = ysum_mid(links, cs, csrc.at[0], cbuf.at[0], cres.at[0])
+    cs = half_mid(links, cs, cparts, chead, hsem, cres)
     state = factor_some(8, 12, state)
     low, nt_, inv = factor_end(state)
     unit = unit_part(low, B)
     kr = make_k(unit, 0)
 
     def image(lanes):
-        yy[:, lanes] = nn(low, wc[1, :, lanes]) - yc[0, :, lanes]
+        yy[:, lanes] = nn(low, wc[1, :, lanes]) - im[:, lanes]
     chunks(image)
     es = ysum_mid(links, es, esrc, ebuf, eres)
     w2 = z_in(2)
     arrive(rs)
     arrive(wr_hi)
-    yrow = rres[0, 0]
+    yrow = rres[0, 0] * scale
     yr = nn(low, wr[1]) - yrow
     arrive(cs)
 
-    yt, phi = cres[0, 0, :, 128:128 + B], cres[0, 0, :, 0:B]
+    yt, phi = cres[:, 128:128 + B], cres[:, 0:B]
     of_k = -nn(inv, nt(nt(yt, low) - phi, nt_))
     of_both = jnp.concatenate([inv, of_k], axis=1)
 
     def next_panel(lanes):
-        pcs[1, :, lanes] = nn(of_both, jnp.concatenate([yc[0, :, lanes], kc[:, lanes]], axis=0))
+        pcs[1, :, lanes] = nn(of_both, jnp.concatenate([im[:, lanes], kc[:, lanes]], axis=0))
     chunks(next_panel)
     pcs[1] = jnp.where(gl_c >= 2 * B, pcs[1], 0.0)
     gsrc[1, 0, :, 0:128] = widen(product_rows(pcs.at[1], pcs.at[1], B))
@@ -550,10 +600,13 @@
     rs = ysum_mid(links, rs, rsrc.at[1], rbuf.at[1], rres.at[1])
     ps = psum_z(links, ps, sumk.at[1], bufx.at[1], sumx.at[1], bufz.at[1])
     arrive(gs)
-    top = gres[1, 0, :, 128:256]
-    state = factor_some(0, 5, factor_start(gres[1, 0, :, 0:128], top))
+    scale = scale_of(gres[1, 0, :, 0:128])
+    pcs[1] = pcs[1] * scale
+    prs[1] = prs[1] * scale
+    top = gres[1, 0, :, 128:256] * scale
+    state = factor_some(0, 5, factor_start(gres[1, 0, :, 0:128] * scale * scale, top))
     arrive(rs)
-    yrow = rres[1, 0]
+    yrow = rres[1, 0] * scale
     none = jnp.zeros((B, ROWS), F32)
     ssrc[:, 0:128] = widen(nt(prs[1], yrow))
     ssrc[:, 128:256] = (jnp.where(row == 0, square(jnp.concatenate([yrow, none], axis=1), 2 * B), 0.0)
@@ -589,14 +642,16 @@
 
     def last(lanes):
         kcl = kc[:, lanes]
-        hcl = nn(of_h, jnp.concatenate([yy[:, lanes] - yc[1, :, lanes], kcl], axis=0))
+        hcl = nn(of_h, jnp.concatenate([yy[:, lanes] - yc[1, :, lanes] * scale, kcl], axis=0))
         o_ref[:, lanes] = o_ref[:, lanes] - nn(left, jnp.concatenate([kcl, hcl], axis=0))
     chunks(last)
 
     @pl.when(y == 0)
     def _():
-        for g, panels in ((0, 1), (1, 2)):
-            links.take(send.at[ysc + g], (NY - 1) * panels * 24 * 128)
+        links.take(send.at[ysc], (NY - 1) * B * ROWS)
+        links.take(send.at[ysc + 1], (NY - 1) * 2 * 24 * 128)
+        links.take(send.at[hsem], (NY - 1) * 48 * 128)
+        links.take(send.at[hsem + 1], (NY - 1) * 48 * 128)
 
     @pl.when(row == 0)
     def _():
@@ -632,10 +687,11 @@
             vmem((3, 48, COLS), F32), vmem((3, 48, 512), F32),
             vmem((2, B, COLS), F32), vmem((2, 48, COLS), F32), vmem((2, 48, COLS), F32),
             vmem((2, NX, 48, 512), F32), vmem((2, 48, 512), F32), vmem((2, NZ, 24, 128), F32), vmem((2, B, COLS), F32),
-            *ysum_buffers((2,), 1), *ysum_buffers((2,), 1), *ysum_buffers((1,), 1), *ysum_buffers((), 2), *ysum_buffers((), 1),
+            *ysum_buffers((2,), 1), *ysum_buffers((2,), 1), vmem((B, 256), F32), vmem((NY, 48, 128), F32), vmem((48, 128), F32), vmem((B, 256), F32),
+            vmem((NY, 48, 128), F32), vmem((48, 128), F32), *ysum_buffers((), 2), *ysum_buffers((), 1),
             vmem((B, 256), F32), vmem((2, 24, 128), F32), vmem((NX, 24, 128), F32), vmem((NZ, 24, 128), F32), vmem((B, 256), F32),
             vmem((2, B, COLS), F32), vmem((2, B, ROWS), F32), vmem((B, COLS), F32), vmem((B, ROWS), F32),
-            vmem((B, COLS), F32), vmem((B, COLS), F32), vmem((B, COLS), F32), vmem((B, 128), F32),
+            vmem((B, COLS), F32), vmem((B, COLS), F32), vmem((B, COLS), F32), vmem((B, COLS), F32), vmem((B, 128), F32),
             vmem((METER, 128), F32),
             pltpu.SemaphoreType.DMA((SEMS,)), pltpu.SemaphoreType.DMA((SEMS,)),
         ],

time: 125 us -> 125 us (level)
  no operation moved by 1% of the time
where the time goes in v5:
time: 125 us; the launch traced here: 124 us
  Pallas kernels  121 us (97%)
  local copies, waits for them, and re-layouts  3.14 us (3%)
    pallas_call x1, Pallas kernels, local(): pl.pallas_call(body, out_shape=jax.ShapeDtypeStruct((ROWS, COLS), F32), i...  121 us
    unnamed x1, local copies, waits for them, and re-layouts  3.14 us

profile of v5, /device:TPU:1, one launch (start us, length us, event | category | flops | bytes accessed | tf_op | source)
XLA Modules:
  0.0 124.2 jit_solution(6935119169541753119)
XLA Ops:
  0.0 121.0 %two_panels.1 = f32[256,2048]{1,0:T(8,128)} custom-call(f32[256,2048]{1,0:T(8,128)} %a_ref.1), custom_call_target="tpu_custom_call" | custom-call | tf_op jit(solution)/shard_map/two_panels/pallas_call | solution.py:680
  121.0 3.1 %copy.3 = f32[256,2048]{1,0:T(8,128)} copy(f32[256,2048]{1,0:T(8,128)} %two_panels.1) | data formatting | bytes 4194304
